TPU v7x, 32 devices: a whole 2x2x4 slice. The times are simulated.
32 devices in a mesh: sta: 8 (over y, x, core), cel: 4 (over z).
Axes of the slice: x: 2, y: 2, z: 4, core: 2. Of those that a mesh axis runs over, the one named last changes fastest.
Arguments:
- station_plane: int32 [2, 32768], P(None, 'sta'), may hold values from 0 to 191
- station_height: int32 [32768], P('sta'), may hold values from 1 to 4
- cell_plane: int32 [2, 8192], P(None, 'cel'), may hold values from 0 to 191
- cell_depth: int32 [8192], P('cel'), may hold values from 0 to 15
- cell_density: float32 [8192], P('cel'), may hold values from 0.4 to 4
- left_before: float32 [16, 32768], P(None, 'sta'), may hold values from -6 to 6
- left_now: float32 [16, 32768], P(None, 'sta'), may hold values from -6 to 6
- right_before: float32 [16, 8192], P(None, 'cel'), may hold values from -6 to 6
Outputs:
- right_blocks: float32 [2, 16, 8192], P(None, None, 'cel')
- left_block: float32 [16, 32768], P(None, 'sta')
- alphas: float32 [2, 16, 16], replicated
- betas: float32 [2, 16, 16], replicated
All inputs are finite; a program needn't handle non-finite values.
Results may differ from a plain program's by a relative error of at most 0.0003.
Values sent between devices are 32-bit elements; how exact they have to be, the bound alone decides.
A program may use at most 64 MiB of HBM per device.

v0:
```python
import jax
import jax.numpy as jnp
from jax import lax
from jax.sharding import PartitionSpec as P

STEPS = 2


GAIN = 4.0
HIGH = lax.Precision.HIGHEST


def kernel_rows(sx, sy, sz, cx, cy, cz, density):
    dx = sx[:, None] - cx[None, :]
    dy = sy[:, None] - cy[None, :]
    dz = sz[:, None] + cz[None, :] + 0.5
    square = dx * dx + dy * dy + dz * dz
    inverse = lax.rsqrt(square)
    inv_two = inverse * inverse
    return (
        GAIN
        * density[None, :]
        * (2.0 * dz * dz - dx * dx - dy * dy)
        * (inv_two * inv_two * inverse)
    )


def matmul(a, b):
    return jnp.dot(a, b, precision=HIGH, preferred_element_type=jnp.float32)


def cell_sum(values):
    return lax.psum(values, "cel")


def station_sum(values):
    return lax.psum(values, "sta")


def orthonormal(block, basis, rows, summer):
    cross, square, basis_gram = summer(
        (matmul(basis, block.T), matmul(block, block.T), matmul(basis, basis.T))
    )
    coef = cross / rows
    rest = block - matmul(coef.T, basis)
    gram = (
        square / rows - 2.0 * matmul(coef.T, coef) + matmul(coef.T, matmul(basis_gram / rows, coef))
    )
    lower = jnp.linalg.cholesky(gram)
    return (jax.scipy.linalg.solve_triangular(lower, rest, lower=True), lower)


def body(
    station_plane,
    station_height,
    cell_plane,
    cell_depth,
    cell_density,
    left_before,
    left_now,
    right_before,
):
    width = left_now.shape[0]
    s_dev = left_now.shape[1]
    c_dev = right_before.shape[1]
    n_sta = lax.axis_size("sta")
    n_cel = lax.axis_size("cel")
    stations = s_dev * n_sta
    cells = c_dev * n_cel
    sx = station_plane[0].astype(jnp.float32)
    sy = station_plane[1].astype(jnp.float32)
    sz = station_height.astype(jnp.float32)
    cx = cell_plane[0].astype(jnp.float32)
    cy = cell_plane[1].astype(jnp.float32)
    cz = cell_depth.astype(jnp.float32)
    block = 512
    count = s_dev // block

    def tile_at(start):
        a = lax.dynamic_slice_in_dim(sx, start, block)
        b = lax.dynamic_slice_in_dim(sy, start, block)
        c = lax.dynamic_slice_in_dim(sz, start, block)
        return kernel_rows(a, b, c, cx, cy, cz, cell_density)

    right_basis = right_before
    left_basis = jnp.concatenate([left_before, left_now], 0)
    left = left_now
    rights, alphas, betas = ([], [], [])
    for step in range(STEPS):

        def add_block(index, total):
            start = index * block
            rows = lax.dynamic_slice_in_dim(left, start, block, 1)
            return total + matmul(rows, tile_at(start))

        adjoint_terms = lax.fori_loop(0, count, add_block, jnp.zeros((width, c_dev), jnp.float32))
        whole = lax.psum(adjoint_terms, "sta")
        right, alpha = orthonormal(whole, right_basis, cells, cell_sum)
        right_basis = jnp.concatenate([right_basis, right], 0)

        def one_block(index):
            return lax.dot_general(
                right,
                tile_at(index * block),
                (((1,), (1,)), ((), ())),
                precision=HIGH,
                preferred_element_type=jnp.float32,
            )

        parts = lax.map(one_block, jnp.arange(count))
        forward_terms = parts.transpose(1, 0, 2).reshape(width, s_dev)
        whole_left = lax.psum(forward_terms, "cel")
        left, beta = orthonormal(whole_left, left_basis, stations, station_sum)
        left_basis = jnp.concatenate([left_basis, left], 0)
        rights.append(right)
        alphas.append(alpha)
        betas.append(beta)
    return (jnp.stack(rights), left, jnp.stack(alphas), jnp.stack(betas))


def solution(mesh):
    in_specs = (
        P(None, "sta"),
        P("sta"),
        P(None, "cel"),
        P("cel"),
        P("cel"),
        P(None, "sta"),
        P(None, "sta"),
        P(None, "cel"),
    )
    out_specs = (P(None, None, "cel"), P(None, "sta"), P(), P())
    return jax.shard_map(body, mesh=mesh, in_specs=in_specs, out_specs=out_specs, check_vma=False)
```

profile of v0, /device:TPU:0, one launch (start us, length us, event | category | flops | bytes accessed | tf_op | source)
XLA Modules:
  0.0 520.0 jit_solution(2808148154138339772)
XLA Ops:
  7.2 0.9 slice_convert_fusion
  8.1 0.8 slice_convert_fusion.2
  8.9 0.7 convert_element_type.30
  10.3 51.1 %while.50 = (s32[]{:T(128)}, f32[16,2048]{1,0:T(8,128)S(1)}, f32[16,4096]{1,0:T(8,128)}, f32[2048]{0:T(1024)}, f32[4096]{0:T(1024)S(1)}, /*index=5*/f32[2048]{0:...) while((s32[]{:T(128)}, f32[16,2048]{1,0:T(8,128)S(1)}, ...), condition=%wide.region_1.0_spmd.clone, body=%wide.region_0.0_spmd.clone.sunk | while | flops 220268544 | bytes 362701 | solution.py:96
  11.2 5.5 %fusion.289 = f32[16,2048]{1,0:T(8,128)S(1)} fusion(f32[2048]{0:T(1024)S(1)} %get-tuple-element.930, f32[512]{0:T(512)S(1)} %dynamic_slice.118, f32[2048]{0:T(1024)S(1)} %get-tuple-element.928, f32[512]{0:T(512)S(1)} %dynamic_slice.119, f32[2048]{0:T(1024)S(1)} %get-tuple-element.926, f32[512]{0:T(512)S(1)} %dynamic_slice.120, ...), kind=kOutput, calls=%fused_computation.85.clone.1 | convolution fusion | flops 220266496 | bytes 333829 | tf_op jit(solution)/shard_map/while/body/eval_jaxpr/dot_general | solution.py:29
  17.6 5.5 %fusion.289 = f32[16,2048]{1,0:T(8,128)S(1)} fusion(f32[2048]{0:T(1024)S(1)} %get-tuple-element.930, f32[512]{0:T(512)S(1)} %dynamic_slice.118, f32[2048]{0:T(1024)S(1)} %get-tuple-element.928, f32[512]{0:T(512)S(1)} %dynamic_slice.119, f32[2048]{0:T(1024)S(1)} %get-tuple-element.926, f32[512]{0:T(512)S(1)} %dynamic_slice.120, ...), kind=kOutput, calls=%fused_computation.85.clone.1 | convolution fusion | flops 220266496 | bytes 333829 | tf_op jit(solution)/shard_map/while/body/eval_jaxpr/dot_general | solution.py:29
  24.0 5.5 %fusion.289 = f32[16,2048]{1,0:T(8,128)S(1)} fusion(f32[2048]{0:T(1024)S(1)} %get-tuple-element.930, f32[512]{0:T(512)S(1)} %dynamic_slice.118, f32[2048]{0:T(1024)S(1)} %get-tuple-element.928, f32[512]{0:T(512)S(1)} %dynamic_slice.119, f32[2048]{0:T(1024)S(1)} %get-tuple-element.926, f32[512]{0:T(512)S(1)} %dynamic_slice.120, ...), kind=kOutput, calls=%fused_computation.85.clone.1 | convolution fusion | flops 220266496 | bytes 333829 | tf_op jit(solution)/shard_map/while/body/eval_jaxpr/dot_general | solution.py:29
  30.4 5.5 %fusion.289 = f32[16,2048]{1,0:T(8,128)S(1)} fusion(f32[2048]{0:T(1024)S(1)} %get-tuple-element.930, f32[512]{0:T(512)S(1)} %dynamic_slice.118, f32[2048]{0:T(1024)S(1)} %get-tuple-element.928, f32[512]{0:T(512)S(1)} %dynamic_slice.119, f32[2048]{0:T(1024)S(1)} %get-tuple-element.926, f32[512]{0:T(512)S(1)} %dynamic_slice.120, ...), kind=kOutput, calls=%fused_computation.85.clone.1 | convolution fusion | flops 220266496 | bytes 333829 | tf_op jit(solution)/shard_map/while/body/eval_jaxpr/dot_general | solution.py:29
  36.8 5.5 %fusion.289 = f32[16,2048]{1,0:T(8,128)S(1)} fusion(f32[2048]{0:T(1024)S(1)} %get-tuple-element.930, f32[512]{0:T(512)S(1)} %dynamic_slice.118, f32[2048]{0:T(1024)S(1)} %get-tuple-element.928, f32[512]{0:T(512)S(1)} %dynamic_slice.119, f32[2048]{0:T(1024)S(1)} %get-tuple-element.926, f32[512]{0:T(512)S(1)} %dynamic_slice.120, ...), kind=kOutput, calls=%fused_computation.85.clone.1 | convolution fusion | flops 220266496 | bytes 333829 | tf_op jit(solution)/shard_map/while/body/eval_jaxpr/dot_general | solution.py:29
  43.2 5.5 %fusion.289 = f32[16,2048]{1,0:T(8,128)S(1)} fusion(f32[2048]{0:T(1024)S(1)} %get-tuple-element.930, f32[512]{0:T(512)S(1)} %dynamic_slice.118, f32[2048]{0:T(1024)S(1)} %get-tuple-element.928, f32[512]{0:T(512)S(1)} %dynamic_slice.119, f32[2048]{0:T(1024)S(1)} %get-tuple-element.926, f32[512]{0:T(512)S(1)} %dynamic_slice.120, ...), kind=kOutput, calls=%fused_computation.85.clone.1 | convolution fusion | flops 220266496 | bytes 333829 | tf_op jit(solution)/shard_map/while/body/eval_jaxpr/dot_general | solution.py:29
  49.6 5.5 %fusion.289 = f32[16,2048]{1,0:T(8,128)S(1)} fusion(f32[2048]{0:T(1024)S(1)} %get-tuple-element.930, f32[512]{0:T(512)S(1)} %dynamic_slice.118, f32[2048]{0:T(1024)S(1)} %get-tuple-element.928, f32[512]{0:T(512)S(1)} %dynamic_slice.119, f32[2048]{0:T(1024)S(1)} %get-tuple-element.926, f32[512]{0:T(512)S(1)} %dynamic_slice.120, ...), kind=kOutput, calls=%fused_computation.85.clone.1 | convolution fusion | flops 220266496 | bytes 333829 | tf_op jit(solution)/shard_map/while/body/eval_jaxpr/dot_general | solution.py:29
  56.0 5.5 %fusion.289 = f32[16,2048]{1,0:T(8,128)S(1)} fusion(f32[2048]{0:T(1024)S(1)} %get-tuple-element.930, f32[512]{0:T(512)S(1)} %dynamic_slice.118, f32[2048]{0:T(1024)S(1)} %get-tuple-element.928, f32[512]{0:T(512)S(1)} %dynamic_slice.119, f32[2048]{0:T(1024)S(1)} %get-tuple-element.926, f32[512]{0:T(512)S(1)} %dynamic_slice.120, ...), kind=kOutput, calls=%fused_computation.85.clone.1 | convolution fusion | flops 220266496 | bytes 333829 | tf_op jit(solution)/shard_map/while/body/eval_jaxpr/dot_general | solution.py:29
  63.3 54.6 %all-reduce.9.cloned.1.call-done = f32[16,2048]{1,0:T(8,128)} async-done(((f32[16,2048]{1,0:T(8,128)}), f32[16,2048]{1,0:T(8,128)}) %all-reduce.9.cloned.1.call-update) | async-done | bytes 131088 | tf_op jit(solution)/shard_map/psum | solution.py:97
  117.9 1.2 convolution_bitcast_fusion
  119.1 1.3 fusion.232
  120.4 19.0 %all-reduce.3 = (f32[16,16]{0,1:T(8,128)S(1)}, f32[16,16]{0,1:T(8,128)S(1)}, f32[16,16]{0,1:T(8,128)S(1)}) all-reduce(f32[16,16]{0,1:T(8,128)S(1)} %convolution_bitcast_fusion, f32[16,16]{0,1:T(8,128)S(1)} %fusion.232, f32[16,16]{0,1:T(8,128)S(1)} %fusion.233), channel_id=1, replica_groups=mesh['sta'=8,'cel'=4] {'cel'}, use_global_device_ids=true, to_apply=%region_4.0 | all-reduce | flops 768 | bytes 6144 | tf_op jit(solution)/shard_map/psum | solution.py:33
  140.0 1.5 cholesky.74
  142.8 1.2 custom-call.12
  144.7 61.5 %while.48 = (s32[]{:T(128)}, f32[8,16,512]{2,1,0:T(8,128)S(1)}, f32[2048]{0:T(1024)S(1)}, s32[8]{0:T(128)S(1)}, f32[4096]{0:T(1024)S(1)}, /*index=5*/f32[2048]{0...) while((s32[]{:T(128)}, f32[8,16,512]{2,1,0:T(8,128)S(1)}, ...), condition=%wide.region_9.12_spmd, body=%wide.region_8.11_spmd.sunk | while | flops 220203008 | bytes 231639 | solution.py:110
  146.2 6.2 %fusion.283 = f32[8,16,512]{2,1,0:T(8,128)S(1)} fusion(f32[8,16,512]{2,1,0:T(8,128)S(1)} %get-tuple-element.951, s32[]{:T(128)} %get-tuple-element.950, f32[16,2048]{1,0:T(8,128)S(1)} %get-tuple-element.975, f32[2048]{0:T(1024)S(1)} %get-tuple-element.974, f32[512]{0:T(512)S(1)} %dynamic_slice.110, f32[2048]{0:T(1024)S(1)} %get-tuple-element.972, ...), kind=kOutput, calls=%fused_computation.29.clone.1 | convolution fusion | flops 220200960 | bytes 202756 | tf_op jit(solution)/shard_map/while/body/eval_jaxpr/dot_general | solution.py:102
  153.9 6.2 %fusion.283 = f32[8,16,512]{2,1,0:T(8,128)S(1)} fusion(f32[8,16,512]{2,1,0:T(8,128)S(1)} %get-tuple-element.951, s32[]{:T(128)} %get-tuple-element.950, f32[16,2048]{1,0:T(8,128)S(1)} %get-tuple-element.975, f32[2048]{0:T(1024)S(1)} %get-tuple-element.974, f32[512]{0:T(512)S(1)} %dynamic_slice.110, f32[2048]{0:T(1024)S(1)} %get-tuple-element.972, ...), kind=kOutput, calls=%fused_computation.29.clone.1 | convolution fusion | flops 220200960 | bytes 202756 | tf_op jit(solution)/shard_map/while/body/eval_jaxpr/dot_general | solution.py:102
  161.5 6.2 %fusion.283 = f32[8,16,512]{2,1,0:T(8,128)S(1)} fusion(f32[8,16,512]{2,1,0:T(8,128)S(1)} %get-tuple-element.951, s32[]{:T(128)} %get-tuple-element.950, f32[16,2048]{1,0:T(8,128)S(1)} %get-tuple-element.975, f32[2048]{0:T(1024)S(1)} %get-tuple-element.974, f32[512]{0:T(512)S(1)} %dynamic_slice.110, f32[2048]{0:T(1024)S(1)} %get-tuple-element.972, ...), kind=kOutput, calls=%fused_computation.29.clone.1 | convolution fusion | flops 220200960 | bytes 202756 | tf_op jit(solution)/shard_map/while/body/eval_jaxpr/dot_general | solution.py:102
  169.2 6.2 %fusion.283 = f32[8,16,512]{2,1,0:T(8,128)S(1)} fusion(f32[8,16,512]{2,1,0:T(8,128)S(1)} %get-tuple-element.951, s32[]{:T(128)} %get-tuple-element.950, f32[16,2048]{1,0:T(8,128)S(1)} %get-tuple-element.975, f32[2048]{0:T(1024)S(1)} %get-tuple-element.974, f32[512]{0:T(512)S(1)} %dynamic_slice.110, f32[2048]{0:T(1024)S(1)} %get-tuple-element.972, ...), kind=kOutput, calls=%fused_computation.29.clone.1 | convolution fusion | flops 220200960 | bytes 202756 | tf_op jit(solution)/shard_map/while/body/eval_jaxpr/dot_general | solution.py:102
  176.9 6.2 %fusion.283 = f32[8,16,512]{2,1,0:T(8,128)S(1)} fusion(f32[8,16,512]{2,1,0:T(8,128)S(1)} %get-tuple-element.951, s32[]{:T(128)} %get-tuple-element.950, f32[16,2048]{1,0:T(8,128)S(1)} %get-tuple-element.975, f32[2048]{0:T(1024)S(1)} %get-tuple-element.974, f32[512]{0:T(512)S(1)} %dynamic_slice.110, f32[2048]{0:T(1024)S(1)} %get-tuple-element.972, ...), kind=kOutput, calls=%fused_computation.29.clone.1 | convolution fusion | flops 220200960 | bytes 202756 | tf_op jit(solution)/shard_map/while/body/eval_jaxpr/dot_general | solution.py:102
  184.6 6.2 %fusion.283 = f32[8,16,512]{2,1,0:T(8,128)S(1)} fusion(f32[8,16,512]{2,1,0:T(8,128)S(1)} %get-tuple-element.951, s32[]{:T(128)} %get-tuple-element.950, f32[16,2048]{1,0:T(8,128)S(1)} %get-tuple-element.975, f32[2048]{0:T(1024)S(1)} %get-tuple-element.974, f32[512]{0:T(512)S(1)} %dynamic_slice.110, f32[2048]{0:T(1024)S(1)} %get-tuple-element.972, ...), kind=kOutput, calls=%fused_computation.29.clone.1 | convolution fusion | flops 220200960 | bytes 202756 | tf_op jit(solution)/shard_map/while/body/eval_jaxpr/dot_general | solution.py:102
  192.3 6.2 %fusion.283 = f32[8,16,512]{2,1,0:T(8,128)S(1)} fusion(f32[8,16,512]{2,1,0:T(8,128)S(1)} %get-tuple-element.951, s32[]{:T(128)} %get-tuple-element.950, f32[16,2048]{1,0:T(8,128)S(1)} %get-tuple-element.975, f32[2048]{0:T(1024)S(1)} %get-tuple-element.974, f32[512]{0:T(512)S(1)} %dynamic_slice.110, f32[2048]{0:T(1024)S(1)} %get-tuple-element.972, ...), kind=kOutput, calls=%fused_computation.29.clone.1 | convolution fusion | flops 220200960 | bytes 202756 | tf_op jit(solution)/shard_map/while/body/eval_jaxpr/dot_general | solution.py:102
  199.9 6.2 %fusion.283 = f32[8,16,512]{2,1,0:T(8,128)S(1)} fusion(f32[8,16,512]{2,1,0:T(8,128)S(1)} %get-tuple-element.951, s32[]{:T(128)} %get-tuple-element.950, f32[16,2048]{1,0:T(8,128)S(1)} %get-tuple-element.975, f32[2048]{0:T(1024)S(1)} %get-tuple-element.974, f32[512]{0:T(512)S(1)} %dynamic_slice.110, f32[2048]{0:T(1024)S(1)} %get-tuple-element.972, ...), kind=kOutput, calls=%fused_computation.29.clone.1 | convolution fusion | flops 220200960 | bytes 202756 | tf_op jit(solution)/shard_map/while/body/eval_jaxpr/dot_general | solution.py:102
  206.1 0.7 copy.58
  207.9 31.2 %all-reduce.11.cloned.1.call-done = f32[16,4096]{1,0:T(8,128)} async-done(((f32[16,4096]{1,0:T(8,128)}), f32[16,4096]{1,0:T(8,128)}) %all-reduce.11.cloned.1.call-update) | async-done | bytes 262160 | tf_op jit(solution)/shard_map/psum | solution.py:112
  239.1 1.5 fusion.235
  241.1 22.7 %all-reduce.1 = (f32[32,16]{0,1:T(8,128)S(1)}, f32[16,16]{0,1:T(8,128)S(1)}, f32[32,32]{1,0:T(8,128)S(1)}) all-reduce(f32[32,16]{0,1:T(8,128)S(1)} %fusion.235, f32[16,16]{0,1:T(8,128)S(1)} %fusion.234, f32[32,32]{1,0:T(8,128)S(1)} %fusion.236), channel_id=1, replica_groups=mesh['sta'=8,'cel'=4] {'sta'}, use_global_device_ids=true, to_apply=%region_12.15 | all-reduce | flops 1792 | bytes 14336 | tf_op jit(solution)/shard_map/psum | solution.py:37
  264.3 1.5 cholesky.85
  267.1 1.2 custom-call.13
  269.2 39.5 %while.51 = (s32[]{:T(128)}, f32[16,2048]{1,0:T(8,128)S(1)}, f32[16,4096]{1,0:T(8,128)S(1)}, f32[2048]{0:T(1024)S(1)}, f32[4096]{0:T(1024)S(1)}, /*index=5*/f32[...) while((s32[]{:T(128)}, f32[16,2048]{1,0:T(8,128)S(1)}, ...), condition=%wide.region_15.19_spmd.clone, body=%wide.region_14.18_spmd.clone.sunk | while | flops 220268544 | bytes 362701 | solution.py:96
  269.4 4.7 fusion.292
  274.3 4.7 fusion.292
  279.3 4.7 fusion.292
  284.2 4.7 fusion.292
  289.1 4.7 fusion.292
  294.1 4.7 fusion.292
  299.0 4.7 fusion.292
  303.9 4.7 fusion.292
  309.4 0.8 fusion.146
  310.2 51.1 %all-reduce.13.cloned.1.call-done = f32[16,2048]{1,0:T(8,128)} async-done(((f32[16,2048]{1,0:T(8,128)}), f32[16,2048]{1,0:T(8,128)}) %all-reduce.13.cloned.1.call-update) | async-done | bytes 131088 | tf_op jit(solution)/shard_map/psum | solution.py:97
  361.2 1.3 fusion.149
  362.8 19.1 %all-reduce.2 = (f32[32,16]{0,1:T(8,128)S(1)}, f32[16,16]{0,1:T(8,128)S(1)}, f32[32,32]{1,0:T(8,128)S(1)}) all-reduce(f32[32,16]{0,1:T(8,128)S(1)} %fusion.149, f32[16,16]{0,1:T(8,128)S(1)} %fusion.237, f32[32,32]{1,0:T(8,128)S(1)} %fusion.148), channel_id=1, replica_groups=mesh['sta'=8,'cel'=4] {'cel'}, use_global_device_ids=true, to_apply=%region_18.22 | all-reduce | flops 1792 | bytes 14336 | tf_op jit(solution)/shard_map/psum | solution.py:33
  382.4 1.5 cholesky.96
  385.2 1.2 custom-call.14
  387.1 61.5 %while.49 = (s32[]{:T(128)}, f32[8,16,512]{2,1,0:T(8,128)S(1)}, f32[2048]{0:T(1024)S(1)}, s32[8]{0:T(128)S(1)}, f32[4096]{0:T(1024)S(1)}, /*index=5*/f32[2048]{0...) while((s32[]{:T(128)}, f32[8,16,512]{2,1,0:T(8,128)S(1)}, ...), condition=%wide.region_21.25_spmd, body=%wide.region_20.24_spmd.sunk | while | flops 220203008 | bytes 231639 | solution.py:110
  388.6 6.2 %fusion.286 = f32[8,16,512]{2,1,0:T(8,128)S(1)} fusion(f32[8,16,512]{2,1,0:T(8,128)S(1)} %get-tuple-element.1038, s32[]{:T(128)} %get-tuple-element.1037, f32[16,2048]{1,0:T(8,128)S(1)} %get-tuple-element.1062, f32[2048]{0:T(1024)S(1)} %get-tuple-element.1061, f32[512]{0:T(512)S(1)} %dynamic_slice.114, f32[2048]{0:T(1024)S(1)} %get-tuple-element.1059, ...), kind=kOutput, calls=%fused_computation.62.clone.1 | convolution fusion | flops 220200960 | bytes 202756 | tf_op jit(solution)/shard_map/while/body/eval_jaxpr/dot_general | solution.py:102
  396.2 6.2 %fusion.286 = f32[8,16,512]{2,1,0:T(8,128)S(1)} fusion(f32[8,16,512]{2,1,0:T(8,128)S(1)} %get-tuple-element.1038, s32[]{:T(128)} %get-tuple-element.1037, f32[16,2048]{1,0:T(8,128)S(1)} %get-tuple-element.1062, f32[2048]{0:T(1024)S(1)} %get-tuple-element.1061, f32[512]{0:T(512)S(1)} %dynamic_slice.114, f32[2048]{0:T(1024)S(1)} %get-tuple-element.1059, ...), kind=kOutput, calls=%fused_computation.62.clone.1 | convolution fusion | flops 220200960 | bytes 202756 | tf_op jit(solution)/shard_map/while/body/eval_jaxpr/dot_general | solution.py:102
  403.9 6.2 %fusion.286 = f32[8,16,512]{2,1,0:T(8,128)S(1)} fusion(f32[8,16,512]{2,1,0:T(8,128)S(1)} %get-tuple-element.1038, s32[]{:T(128)} %get-tuple-element.1037, f32[16,2048]{1,0:T(8,128)S(1)} %get-tuple-element.1062, f32[2048]{0:T(1024)S(1)} %get-tuple-element.1061, f32[512]{0:T(512)S(1)} %dynamic_slice.114, f32[2048]{0:T(1024)S(1)} %get-tuple-element.1059, ...), kind=kOutput, calls=%fused_computation.62.clone.1 | convolution fusion | flops 220200960 | bytes 202756 | tf_op jit(solution)/shard_map/while/body/eval_jaxpr/dot_general | solution.py:102
  411.6 6.2 %fusion.286 = f32[8,16,512]{2,1,0:T(8,128)S(1)} fusion(f32[8,16,512]{2,1,0:T(8,128)S(1)} %get-tuple-element.1038, s32[]{:T(128)} %get-tuple-element.1037, f32[16,2048]{1,0:T(8,128)S(1)} %get-tuple-element.1062, f32[2048]{0:T(1024)S(1)} %get-tuple-element.1061, f32[512]{0:T(512)S(1)} %dynamic_slice.114, f32[2048]{0:T(1024)S(1)} %get-tuple-element.1059, ...), kind=kOutput, calls=%fused_computation.62.clone.1 | convolution fusion | flops 220200960 | bytes 202756 | tf_op jit(solution)/shard_map/while/body/eval_jaxpr/dot_general | solution.py:102
  419.3 6.2 %fusion.286 = f32[8,16,512]{2,1,0:T(8,128)S(1)} fusion(f32[8,16,512]{2,1,0:T(8,128)S(1)} %get-tuple-element.1038, s32[]{:T(128)} %get-tuple-element.1037, f32[16,2048]{1,0:T(8,128)S(1)} %get-tuple-element.1062, f32[2048]{0:T(1024)S(1)} %get-tuple-element.1061, f32[512]{0:T(512)S(1)} %dynamic_slice.114, f32[2048]{0:T(1024)S(1)} %get-tuple-element.1059, ...), kind=kOutput, calls=%fused_computation.62.clone.1 | convolution fusion | flops 220200960 | bytes 202756 | tf_op jit(solution)/shard_map/while/body/eval_jaxpr/dot_general | solution.py:102
  427.0 6.2 %fusion.286 = f32[8,16,512]{2,1,0:T(8,128)S(1)} fusion(f32[8,16,512]{2,1,0:T(8,128)S(1)} %get-tuple-element.1038, s32[]{:T(128)} %get-tuple-element.1037, f32[16,2048]{1,0:T(8,128)S(1)} %get-tuple-element.1062, f32[2048]{0:T(1024)S(1)} %get-tuple-element.1061, f32[512]{0:T(512)S(1)} %dynamic_slice.114, f32[2048]{0:T(1024)S(1)} %get-tuple-element.1059, ...), kind=kOutput, calls=%fused_computation.62.clone.1 | convolution fusion | flops 220200960 | bytes 202756 | tf_op jit(solution)/shard_map/while/body/eval_jaxpr/dot_general | solution.py:102
  434.7 6.2 %fusion.286 = f32[8,16,512]{2,1,0:T(8,128)S(1)} fusion(f32[8,16,512]{2,1,0:T(8,128)S(1)} %get-tuple-element.1038, s32[]{:T(128)} %get-tuple-element.1037, f32[16,2048]{1,0:T(8,128)S(1)} %get-tuple-element.1062, f32[2048]{0:T(1024)S(1)} %get-tuple-element.1061, f32[512]{0:T(512)S(1)} %dynamic_slice.114, f32[2048]{0:T(1024)S(1)} %get-tuple-element.1059, ...), kind=kOutput, calls=%fused_computation.62.clone.1 | convolution fusion | flops 220200960 | bytes 202756 | tf_op jit(solution)/shard_map/while/body/eval_jaxpr/dot_general | solution.py:102
  442.3 6.2 %fusion.286 = f32[8,16,512]{2,1,0:T(8,128)S(1)} fusion(f32[8,16,512]{2,1,0:T(8,128)S(1)} %get-tuple-element.1038, s32[]{:T(128)} %get-tuple-element.1037, f32[16,2048]{1,0:T(8,128)S(1)} %get-tuple-element.1062, f32[2048]{0:T(1024)S(1)} %get-tuple-element.1061, f32[512]{0:T(512)S(1)} %dynamic_slice.114, f32[2048]{0:T(1024)S(1)} %get-tuple-element.1059, ...), kind=kOutput, calls=%fused_computation.62.clone.1 | convolution fusion | flops 220200960 | bytes 202756 | tf_op jit(solution)/shard_map/while/body/eval_jaxpr/dot_general | solution.py:102
  448.5 0.7 copy.59
  450.6 30.8 %all-reduce.15.cloned.1.call-done = f32[16,4096]{1,0:T(8,128)} async-done(((f32[16,4096]{1,0:T(8,128)}), f32[16,4096]{1,0:T(8,128)}) %all-reduce.15.cloned.1.call-update) | async-done | bytes 262160 | tf_op jit(solution)/shard_map/psum | solution.py:112
  481.4 1.7 fusion.147
  483.6 23.0 %all-reduce = (f32[48,16]{0,1:T(8,128)S(1)}, f32[16,16]{0,1:T(8,128)S(1)}, f32[48,48]{1,0:T(8,128)S(1)}) all-reduce(f32[48,16]{0,1:T(8,128)S(1)} %fusion.147, f32[16,16]{0,1:T(8,128)S(1)} %fusion.238, f32[48,48]{1,0:T(8,128)S(1)} %fusion.146), channel_id=1, replica_groups=mesh['sta'=8,'cel'=4] {'sta'}, use_global_device_ids=true, to_apply=%region_24.28 | all-reduce | flops 3328 | bytes 26624 | tf_op jit(solution)/shard_map/psum | solution.py:37
  507.2 1.5 cholesky.107
  510.0 1.2 custom-call.15
  512.4 1.1 fusion.157
  (229 shorter events, 40.1 us)
Async XLA Ops:
  7.2 110.7 %all-reduce.9.cloned.1.call-start = ((), (), s32[]{:S(2)}) async-start(), calls=%async_computation | async-start | bytes 262144 | tf_op jit(solution)/shard_map/psum | solution.py:97
  10.3 51.8 %copy-start.5 = (f32[16,4096]{1,0:T(8,128)S(1)}, f32[16,4096]{1,0:T(8,128)}, u32[]{:S(2)}) copy-start(f32[16,4096]{1,0:T(8,128)} %param.26) | copy-start | bytes 786436
  61.4 0.7 copy-start.9
  61.4 1.0 copy-start.4
  62.1 0.9 copy-start
  62.1 176.9 %all-reduce.11.cloned.1.call-start = ((), (), s32[]{:S(2)}) async-start(), calls=%async_computation.1 | async-start | bytes 524288 | tf_op jit(solution)/shard_map/psum | solution.py:112
  117.9 26.2 %copy-start.6 = (f32[16,2048]{1,0:T(8,128)S(1)}, f32[16,2048]{1,0:T(8,128)}, u32[]{:S(2)}) copy-start(f32[16,2048]{1,0:T(8,128)} %all-reduce.9.cloned.1.call-done) | copy-start | bytes 393220
  139.7 5.0 copy-start.3
  206.9 154.3 %all-reduce.13.cloned.1.call-start = ((), (), s32[]{:S(2)}) async-start(), calls=%async_computation.2 | async-start | bytes 262144 | tf_op jit(solution)/shard_map/psum | solution.py:97
  239.1 1.6 copy-start.2
  308.7 0.7 copy-start.8
  309.3 172.1 %all-reduce.15.cloned.1.call-start = ((), (), s32[]{:S(2)}) async-start(), calls=%async_computation.3 | async-start | bytes 524288 | tf_op jit(solution)/shard_map/psum | solution.py:112
  361.2 1.3 copy-start.7
  481.4 1.7 copy-start.1
Sparse Core Ops, SparseCore 0:
  62.2 55.6 all-reduce.8
  207.0 31.9 all-reduce.10
  309.5 51.7 all-reduce.12
  449.4 31.9 all-reduce.14
where the time goes:
time: 522 us; the launch traced here: 520 us
  matrix products  196 us (38%)
  waiting for transfers between devices  168 us (32%)
  blocking collectives  83.8 us (16%)
  other arithmetic  26.8 us (5%)
  local copies, waits for them, and re-layouts  20.8 us (4%)
  between operations  14.1 us (3%)
  loops' own time  10.7 us (2%)
    psum x2, waiting for transfers between devices, body(): whole = lax.psum(adjoint_terms, 'sta')  106 us
    dot_general x16, matrix products, one_block(): lax.dot_general(right, tile_at(index * block), (((1,), (1,)), ((), ())),...  99 us
    dot_general x44, matrix products, matmul(): return jnp.dot(a, b, precision=HIGH, preferred_element_type=jnp.float32)  94.8 us
    psum x2, waiting for transfers between devices, body(): whole_left = lax.psum(forward_terms, 'cel')  62 us
    psum x2, blocking collectives, station_sum(): return lax.psum(values, 'sta')  45.7 us
    psum x2, blocking collectives, cell_sum(): return lax.psum(values, 'cel')  38.1 us
    another operation x2, loops' own time, body(): parts = lax.map(one_block, jnp.arange(count))  10.6 us
  transfers between devices with their start and end apart: 4, of which 4 were waited for; matrix products, arithmetic and copies ran while one was open for 1% of the time, Pallas kernels for 0%

commit v1 on v0

v1 whole, which is shorter than its diff:
```python
import functools

import jax
import jax.numpy as jnp
from jax import lax
from jax.experimental import pallas as pl
from jax.experimental.pallas import tpu as pltpu
from jax.sharding import PartitionSpec as P

STEPS = 2
GAIN = 4.0
CENTER = 96.0
FEATURES = 16
HIGH = lax.Precision.HIGHEST
F32 = jnp.float32
BF16 = jnp.bfloat16
MESH = pl.DeviceIdType.MESH
NN = (((1,), (0,)), ((), ()))
NT = (((1,), (1,)), ((), ()))
TN = (((0,), (0,)), ((), ()))


def dot(a, b, dims, precision=None):
    return lax.dot_general(a, b, dims, precision=precision, preferred_element_type=F32)


def split(values):
    high = values.astype(BF16)
    return high, (values - high.astype(F32)).astype(BF16)


def station_features(plane, height):
    x = plane[0].astype(F32) - CENTER
    y = plane[1].astype(F32) - CENTER
    z = height.astype(F32)
    flat = x * x + y * y
    high = jnp.floor(flat / 256.0) * 256.0
    one = jnp.ones_like(x)
    zero = jnp.zeros_like(x)
    rows = [high, flat - high, one, one, x, y, z * z, z, one, one]
    rows += [zero] * (FEATURES - len(rows))
    return jnp.stack(rows).astype(BF16)


def cell_features(plane, depth):
    x = plane[0].astype(F32) - CENTER
    y = plane[1].astype(F32) - CENTER
    z = depth.astype(F32)
    flat = x * x + y * y
    high = jnp.floor(flat / 256.0) * 256.0
    low = flat - high
    one = jnp.ones_like(x)
    zero = jnp.zeros_like(x)
    pad = [zero] * (FEATURES - 10)
    square = [one, one, high, low, -2.0 * x, -2.0 * y, one, 2.0 * z + one, z * z + z, 0.25 * one]
    top = [-one, -one, -high, -low, 2.0 * x, 2.0 * y, 2.0 * one, 4.0 * z + 2.0 * one]
    top += [2.0 * (z * z + z), 0.5 * one]
    return jnp.stack(square + pad).astype(BF16), jnp.stack(top + pad).astype(BF16)


def eliminate(gram):
    width = gram.shape[0]
    row = lax.broadcasted_iota(jnp.int32, (width, width), 0)
    col = lax.broadcasted_iota(jnp.int32, (width, width), 1)
    eye = (row == col).astype(F32)
    upper, inverse = gram, eye
    for j in range(width - 1):
        pivot = upper[j : j + 1, :]
        factor = jnp.where(row[:, :1] > j, upper[:, j : j + 1] / pivot[:, j : j + 1], 0.0)
        upper = upper - factor * pivot
        inverse = inverse - factor * inverse[j : j + 1, :]
    scale = lax.rsqrt(jnp.sum(eye * upper, axis=1, keepdims=True))
    upper = jnp.where(col >= row, upper * scale, 0.0)
    lower = dot(upper, eye, TN, HIGH)
    return inverse * scale, lower


def combination(sums, basis_gram, rows):
    width = sums.shape[0]
    scaled = sums / rows
    square, coef = scaled[:, :width], scaled[:, width:]
    gram = square - 2.0 * dot(coef, coef, NT, HIGH)
    gram = gram + dot(dot(coef, basis_gram / rows, NN, HIGH), coef, NT, HIGH)
    inverse, lower = eliminate(gram)
    return inverse, coef, lower


def kernel(
    n_sta, n_cel, fs, c_square, c_top, density, before, now, right_before,
    rights, left, alphas, betas,
    g_high, g_low, lhs, gp, forward, rhs, w_full, v_full, z_right, z_left, station_buf, cell_buf,
    small_right, small_left, part,
    sta_send, sta_recv, cel_send, cel_recv, sr_send, sr_recv, sl_send, sl_recv,
):
    width, s_dev = now.shape
    c_dev = right_before.shape[1]
    s_me = lax.axis_index("sta")
    c_me = lax.axis_index("cel")
    cells = float(c_dev * n_cel)
    stations = float(s_dev * n_sta)

    def group(axis):
        me, n = (s_me, n_sta) if axis == "sta" else (c_me, n_cel)
        return [(o, lax.rem(me + o, n)) for o in range(1, n)]

    barrier = pltpu.get_barrier_semaphore()
    for axis in ("sta", "cel"):
        for _, peer in group(axis):
            pl.semaphore_signal(barrier, inc=1, device_id={axis: peer}, device_id_type=MESH)

    def broadcast(axis, source, target, send, recv):
        copies = []
        for o, peer in group(axis):
            copies.append(pltpu.make_async_remote_copy(
                src_ref=source(peer), dst_ref=target, send_sem=send.at[o], recv_sem=recv.at[o],
                device_id={axis: peer}, device_id_type=MESH))
            copies[-1].start()
        return copies

    def finish(copies):
        for copy in copies:
            copy.wait()

    def all_reduce(axis, step, full, buf, send, recv):
        me, n = (s_me, n_sta) if axis == "sta" else (c_me, n_cel)
        share = full.shape[2] // n

        def columns(index):
            return pl.ds(pl.multiple_of(index * share, 128), share)

        mine = columns(me)
        copies = broadcast(
            axis, lambda peer: part.at[:, columns(peer)] if axis == "cel" else gp.at[0, :, columns(peer)],
            buf.at[step, me], send.at[step, 0], recv.at[step, 0])
        own = part[:, mine] if axis == "cel" else gp[0, :, mine]
        finish(copies)
        total = own
        for o, peer in group(axis):
            total = total + buf[step, peer]
        if axis == "sta":
            total = total * density[:, mine]
        full[step, :, mine] = total
        block = full.at[step, :, mine]
        finish(broadcast(axis, lambda peer: block, block, send.at[step, 1], recv.at[step, 1]))

    def small_start(axis, step, z, buf, send, recv):
        me = s_me if axis == "sta" else c_me
        rows = z.shape[0]
        buf[step, me, :rows, :rows] = dot(z, z, NT, HIGH)
        block = buf.at[step, me]
        return broadcast(axis, lambda peer: block, block, send.at[step], recv.at[step])

    def small_end(copies, step, rows, buf):
        finish(copies)
        total = buf[step, 0, :rows, :rows]
        for index in range(1, buf.shape[1]):
            total = total + buf[step, index, :rows, :rows]
        return total

    def mix(inverse, coef, block, basis):
        rest = block
        for index, piece in enumerate(basis):
            rest = rest - dot(coef[:, index * width : (index + 1) * width], piece, NN, HIGH)
        return dot(inverse, rest, NN, HIGH)

    high, low = split(now[...])
    lhs[:width], lhs[2 * width : 3 * width] = high, low
    high, low = split(before[...])
    lhs[width : 2 * width], lhs[3 * width :] = high, low
    gp[...] = jnp.zeros_like(gp)
    s_tile, c_tile = 256, 512
    across = c_dev // c_tile

    def make_tile(index, carry):
        rows = pl.ds(pl.multiple_of(index // across * s_tile, s_tile), s_tile)
        cols = pl.ds(pl.multiple_of(index % across * c_tile, c_tile), c_tile)
        feature = fs[:, rows]
        square = dot(feature, c_square[:, cols], TN)
        top = dot(feature, c_top[:, cols], TN)
        inverse = lax.rsqrt(square)
        two = inverse * inverse
        high, low = split(two * two * (top * inverse))
        g_high[rows, cols] = high
        g_low[rows, cols] = low
        first = dot(lhs[:, rows], high, NN)
        second = dot(lhs[: 2 * width, rows], low, NN)
        for b in range(2):
            gp[b, :, cols] += (
                first[b * width : (b + 1) * width]
                + first[(b + 2) * width : (b + 3) * width]
                + second[b * width : (b + 1) * width]
            )
        return carry

    lax.fori_loop(0, s_dev // s_tile * across, make_tile, 0)
    gp[2] = gp[0]
    pl.semaphore_wait(barrier, n_sta + n_cel - 2)

    left_grams = None
    for step in range(STEPS):
        all_reduce("sta", step, w_full, station_buf, sta_send, sta_recv)
        w = w_full[step]
        z_right[:width] = w
        if step == 0:
            z_right[width : 2 * width] = right_before[...]
        rows = (step + 2) * width
        copies = small_start("cel", step, z_right[:rows], small_right, sr_send, sr_recv)
        high, low = split(w * density[...])
        rhs[:width], rhs[2 * width : 3 * width] = high, low
        if step == 0:
            high, low = split(right_before[...] * density[...])
            rhs[width : 2 * width], rhs[3 * width :] = high, low
        f_tile = 512

        def forward_tile(index, carry):
            span = pl.ds(pl.multiple_of(index * f_tile, f_tile), f_tile)
            first = dot(rhs[...], g_high[span, :], NT)
            second = dot(rhs[: 2 * width], g_low[span, :], NT)
            both = first[: 2 * width] + first[2 * width :] + second
            part[:, span] = both[:width]
            if step == 0:
                forward[0, :, span] = both[width:]
            return carry

        lax.fori_loop(0, s_dev // f_tile, forward_tile, 0)
        sums = small_end(copies, step, rows, small_right)
        inverse, coef, lower = combination(sums[:width], sums[width:, width:], cells)
        alphas[step] = lower
        basis = [z_right[(b + 1) * width : (b + 2) * width] for b in range(step + 1)]
        right = mix(inverse, coef, w, basis)
        rights[step] = right
        values = mix(inverse, coef, part[...], [forward[b] for b in range(step + 1)])
        part[...] = values
        if step + 1 < STEPS:
            z_right[(step + 2) * width : (step + 3) * width] = right
            forward[step + 1] = values

        all_reduce("cel", step, v_full, cell_buf, cel_send, cel_recv)
        v = v_full[step]
        z_left[:width] = v
        if step == 0:
            z_left[width : 2 * width] = before[...]
            z_left[2 * width : 3 * width] = now[...]
        rows = (step + 3) * width
        copies = small_start("sta", step, z_left[:rows], small_left, sl_send, sl_recv)
        if step + 1 < STEPS:
            high, low = split(v)
            lhs[:width], lhs[width : 2 * width] = high, low
            b_tile = 256

            def adjoint_tile(index, carry):
                span = pl.ds(pl.multiple_of(index * b_tile, b_tile), b_tile)
                first = dot(lhs[: 2 * width], g_high[:, span], NN)
                second = dot(lhs[:width], g_low[:, span], NN)
                gp[0, :, span] = first[:width] + first[width:] + second
                return carry

            lax.fori_loop(0, c_dev // b_tile, adjoint_tile, 0)
        sums = small_end(copies, step, rows, small_left)
        inverse, coef, lower = combination(sums[:width], sums[width:, width:], stations)
        betas[step] = lower
        basis = [z_left[(b + 1) * width : (b + 2) * width] for b in range(step + 2)]
        block = mix(inverse, coef, v, basis)
        if step + 1 < STEPS:
            z_left[(step + 3) * width : (step + 4) * width] = block
            values = mix(inverse, coef, gp[0], [gp[b + 1] for b in range(step + 2)])
            gp[0] = values
            if step + 2 < STEPS:
                gp[step + 3] = values
        else:
            left[...] = block


def body(plane, height, cell_plane, depth, density, before, now, right_before):
    width, s_dev = now.shape
    c_dev = right_before.shape[1]
    n_sta = lax.axis_size("sta")
    n_cel = lax.axis_size("cel")
    fs = station_features(plane, height)
    c_square, c_top = cell_features(cell_plane, depth)
    vmem = pl.BlockSpec(memory_space=pltpu.VMEM)
    dma = pltpu.SemaphoreType.DMA
    lanes = 128
    out_shape = (
        jax.ShapeDtypeStruct((STEPS, width, c_dev), F32),
        jax.ShapeDtypeStruct((width, s_dev), F32),
        jax.ShapeDtypeStruct((STEPS, width, width), F32),
        jax.ShapeDtypeStruct((STEPS, width, width), F32),
    )
    scratch = [
        pltpu.VMEM((s_dev, c_dev), BF16),
        pltpu.VMEM((s_dev, c_dev), BF16),
        pltpu.VMEM((4 * width, s_dev), BF16),
        pltpu.VMEM((STEPS + 1, width, c_dev), F32),
        pltpu.VMEM((STEPS, width, s_dev), F32),
        pltpu.VMEM((4 * width, c_dev), BF16),
        pltpu.VMEM((STEPS, width, c_dev), F32),
        pltpu.VMEM((STEPS, width, s_dev), F32),
        pltpu.VMEM(((STEPS + 1) * width, c_dev), F32),
        pltpu.VMEM(((STEPS + 2) * width, s_dev), F32),
        pltpu.VMEM((STEPS, n_sta, width, c_dev // n_sta), F32),
        pltpu.VMEM((STEPS, n_cel, width, s_dev // n_cel), F32),
        pltpu.VMEM((STEPS, n_cel, (STEPS + 1) * width, lanes), F32),
        pltpu.VMEM((STEPS, n_sta, (STEPS + 2) * width, lanes), F32),
        pltpu.VMEM((width, s_dev), F32),
        dma((STEPS, 2, n_sta)),
        dma((STEPS, 2, n_sta)),
        dma((STEPS, 2, n_cel)),
        dma((STEPS, 2, n_cel)),
        dma((STEPS, n_cel)),
        dma((STEPS, n_cel)),
        dma((STEPS, n_sta)),
        dma((STEPS, n_sta)),
    ]
    rights, left, alphas, betas = pl.pallas_call(
        functools.partial(kernel, n_sta, n_cel),
        out_shape=out_shape,
        in_specs=[vmem] * 7,
        out_specs=(vmem,) * 4,
        scratch_shapes=scratch,
        compiler_params=pltpu.CompilerParams(
            collective_id=0, has_side_effects=True, vmem_limit_bytes=56 * 1024 * 1024
        ),
        cost_estimate=pl.CostEstimate(
            flops=2 * 3 * 2 * STEPS * width * s_dev * c_dev, bytes_accessed=4 * 1024 * 1024, transcendentals=s_dev * c_dev
        ),
    )(fs, c_square, c_top, (GAIN * density)[None, :], before, now, right_before)
    return rights, left, alphas, betas


def solution(mesh):
    in_specs = (
        P(None, "sta"),
        P("sta"),
        P(None, "cel"),
        P("cel"),
        P("cel"),
        P(None, "sta"),
        P(None, "sta"),
        P(None, "cel"),
    )
    out_specs = (P(None, None, "cel"), P(None, "sta"), P(), P())
    return jax.shard_map(body, mesh=mesh, in_specs=in_specs, out_specs=out_specs, check_vma=False)
```

time: 522 us -> 141 us (0.27)
  matrix products: 196 us -> 0 us
  waiting for transfers between devices: 168 us -> 0 us
  Pallas kernels: 0 us -> 129 us
  blocking collectives: 83.8 us -> 0 us
  other arithmetic: 26.8 us -> 1.5 us
  between operations: 14.1 us -> 0.82 us
  local copies, waits for them, and re-layouts: 20.8 us -> 9.48 us
  loops' own time: 10.7 us -> 0 us
    dot_general x60 -> x0, matrix products: 194 us -> none  [the longest x16 99 us: one_block(): lax.dot_general(right, tile_at(index * block), (((1,), (1,)), ((), ())),...]
    psum x4 -> x0, waiting for transfers between devices: 168 us -> none  [the longest x2 106 us: body(): whole = lax.psum(adjoint_terms, 'sta')]
    pallas_call x0 -> x1, Pallas kernels: none -> 129 us  [body(): pl.pallas_call(functools.partial(kernel, n_sta, n_cel), out_shape=out_sha...]
    psum x4 -> x0, blocking collectives: 83.8 us -> none  [the longest x2 45.7 us: station_sum(): return lax.psum(values, 'sta')]
    another operation x23 -> x7, other arithmetic: 18 us -> 0.2 us  [the longest x12 8.56 us: orthonormal(): lower = jnp.linalg.cholesky(gram)]
    dynamic_slice x112 -> x0, local copies, waits for them, and re-layouts: 16.8 us -> none  [the longest x16 9.59 us: body(): parts = lax.map(one_block, jnp.arange(count))]
    another operation x4 -> x0, loops' own time: 10.7 us -> none  [the longest x2 10.6 us: body(): parts = lax.map(one_block, jnp.arange(count))]
  transfers between devices with their start and end apart: 4 -> 0, of which waited for: 4 -> 0; matrix products, arithmetic and copies ran while one was open for 1% -> 0% of each run, Pallas kernels for 0% -> 0%
where the time goes in v1:
time: 141 us
  Pallas kernels  129 us (91%)
  local copies, waits for them, and re-layouts  9.48 us (7%)
  other arithmetic  1.5 us (1%)
    pallas_call x1, Pallas kernels, body(): pl.pallas_call(functools.partial(kernel, n_sta, n_cel), out_shape=out_sha...  129 us
    unnamed x18, local copies, waits for them, and re-layouts  5.11 us

profile of v1, /device:TPU:0, one launch (start us, length us, event | category | flops | bytes accessed | tf_op | source)
XLA Modules:
  0.0 140.6 jit_solution(9270977679651075551)
XLA Ops:
  0.6 0.0 copy-start.1
  0.6 1.3 broadcast_multiply_fusion
  1.9 0.0 copy-done.1
  2.0 0.0 copy-start.6
  2.0 0.7 copy-done.6
  2.7 0.0 copy-start.5
  2.8 0.7 copy-done.5
  3.4 0.1 multiply_convert_fusion.2
  3.6 1.3 stack.81.c_top
  5.0 0.0 copy-start.2
  5.0 1.4 stack.76.c_square
  6.4 0.0 copy-done.2
  6.4 0.1 fusion.3
  6.5 1.5 %stack.71.fs = bf16[16,4096]{1,0:T(8,128)(2,1)} concatenate(bf16[1,4096]{1,0:T(2,128)(2,1)S(1)} %fusion.1, bf16[1,4096]{1,0:T(2,128)(2,1)S(1)} %get-tuple-element.10, bf16[2,4096]{1,0:T(2,128)(2,1)S(1)} %broadcast.109, bf16[1,4096]{1,0:T(2,128)(2,1)S(1)} %get-tuple-element.9, bf16[1,4096]{1,0:T(2,128)(2,1)S(1)} %get-tuple-element.8, bf16[1,4096]{1,0:T(2,128)(2,1)S(1)} %stack.67, ...), dimensions={0} | concatenate | bytes 262144 | tf_op jit(solution)/shard_map/stack | solution.py:42
  8.0 128.8 %shard_map.111 = (f32[2,16,2048]{2,1,0:T(8,128)}, f32[16,4096]{1,0:T(8,128)}, f32[2,16,16]{2,1,0:T(8,128)}, f32[2,16,16]{2,1,0:T(8,128)}) custom-call(bf16[16,4096]{1,0:T(8,128)(2,1)} %stack.71.fs, bf16[16,2048]{1,0:T(8,128)(2,1)} %stack.76.c_square, bf16[16,2048]{1,0:T(8,128)(2,1)} %stack.81.c_top, f32[1,2048]{1,0:T(1,128)} %bitcast.1, f32[16,4096]{1,0:T(8,128)} %before.1, ...), custom_call_target="tpu_custom_call" | custom-call | flops 3221225472 | bytes 4194304 | tf_op jit(solution)/shard_map/pallas_call | solution.py:315
  136.8 0.0 copy-start
  136.8 1.7 %copy.16 = f32[2,16,2048]{2,1,0:T(8,128)} copy(f32[2,16,2048]{2,1,0:T(8,128)} %get-tuple-element.29) | data formatting | bytes 524288
  138.5 0.0 copy-done
  138.5 0.0 copy-start.4
  138.5 0.7 copy.17
  139.2 0.0 copy-done.4
  139.2 0.0 copy-start.3
  139.2 0.6 copy.18
  139.9 0.1 copy-done.3
  140.0 0.6 copy.19
  (22 shorter events, 0.2 us)
Async XLA Ops:
  0.6 1.3 copy-start.1
  2.0 0.7 copy-start.6
  2.7 0.7 copy-start.5
  5.0 1.4 copy-start.2
  136.8 1.7 %copy-start = (f32[16,4096]{1,0:T(8,128)S(1)}, f32[16,4096]{1,0:T(8,128)}, u32[]{:S(2)}) copy-start(f32[16,4096]{1,0:T(8,128)} %get-tuple-element.30) | copy-start | bytes 786436
  138.5 0.7 copy-start.4
  139.2 0.7 copy-start.3

commit v2 on v1

v2 whole, which is shorter than its diff:
```python
import functools

import jax
import jax.numpy as jnp
from jax import lax
from jax.experimental import pallas as pl
from jax.experimental.pallas import tpu as pltpu
from jax.sharding import PartitionSpec as P

STEPS = 2
GAIN = 4.0
CENTER = 96.0
FEATURES = 16
HIGH = lax.Precision.HIGHEST
F32 = jnp.float32
BF16 = jnp.bfloat16
MESH = pl.DeviceIdType.MESH
NN = (((1,), (0,)), ((), ()))
NT = (((1,), (1,)), ((), ()))
TN = (((0,), (0,)), ((), ()))


def dot(a, b, dims, precision=None):
    return lax.dot_general(a, b, dims, precision=precision, preferred_element_type=F32)


def split(values):
    high = values.astype(BF16)
    return high, (values - high.astype(F32)).astype(BF16)


def fill_features(ref, rows):
    for index, row in enumerate(rows):
        ref[index : index + 1, :] = row
    ref[len(rows) :, :] = jnp.zeros((FEATURES - len(rows), ref.shape[1]), F32)


def coordinates(plane, level):
    x = plane[0:1, :].astype(F32) - CENTER
    y = plane[1:2, :].astype(F32) - CENTER
    z = level[...].astype(F32)
    flat = x * x + y * y
    high = jnp.floor(flat / 256.0) * 256.0
    return x, y, z, high, flat - high, jnp.ones_like(x)


def station_features(ref, plane, height):
    x, y, z, high, low, one = coordinates(plane, height)
    fill_features(ref, [high, low, one, one, x, y, z * z, z, one, one])


def cell_features(square, top, plane, depth):
    x, y, z, high, low, one = coordinates(plane, depth)
    inner = z * z + z
    rows = [one, one, high, low, -2.0 * x, -2.0 * y, one, 2.0 * z + one, inner, 0.25 * one]
    fill_features(square, rows)
    rows = [-one, -one, -high, -low, 2.0 * x, 2.0 * y, 2.0 * one, 4.0 * z + 2.0 * one]
    fill_features(top, rows + [2.0 * inner, 0.5 * one])


def eliminate(gram):
    width = gram.shape[0]
    row = lax.broadcasted_iota(jnp.int32, (width, width), 0)
    col = lax.broadcasted_iota(jnp.int32, (width, width), 1)
    eye = (row == col).astype(F32)
    upper, inverse = gram, eye
    for j in range(width - 1):
        pivot = upper[j : j + 1, :]
        factor = jnp.where(row[:, :1] > j, upper[:, j : j + 1] / pivot[:, j : j + 1], 0.0)
        upper = upper - factor * pivot
        inverse = inverse - factor * inverse[j : j + 1, :]
    scale = lax.rsqrt(jnp.sum(eye * upper, axis=1, keepdims=True))
    upper = jnp.where(col >= row, upper * scale, 0.0)
    lower = dot(upper, eye, TN, HIGH)
    return inverse * scale, lower


def combination(sums, basis_gram, rows):
    width, total = sums.shape
    scaled = sums / rows
    square, coef = scaled[:, :width], scaled[:, width:]
    span = total - width
    twice = (
        lax.broadcasted_iota(jnp.int32, (span, span), 0)
        == lax.broadcasted_iota(jnp.int32, (span, span), 1)
    )
    inner = jnp.where(twice, 2.0, 0.0) - basis_gram / rows
    gram = square - dot(dot(coef, inner, NN, HIGH), coef, NT, HIGH)
    inverse, lower = eliminate(gram)
    row = lax.broadcasted_iota(jnp.int32, (width, total), 0)
    col = lax.broadcasted_iota(jnp.int32, (width, total), 1)
    weights = dot(inverse, jnp.where(col < width, (row == col).astype(F32), -scaled), NN, HIGH)
    return weights, lower


def self_products(values):
    high, low = split(values)
    return dot(high, high, NT) + dot(high, low, NT) + dot(low, high, NT)


def combine(weights, values):
    width = weights.shape[0]
    high, low = split(values)
    top, bottom = split(weights)
    first = dot(jnp.concatenate([top, bottom], 0), high, NN)
    return first[:width] + first[width:] + dot(top, low, NN)


def kernel(
    n_sta, n_cel, plane, height, cell_plane, depth, density, before, now, right_before,
    rights, left, alphas, betas,
    g_high, g_low, fs, c_square, c_top, lhs, gp, forward, rhs, z_right, z_left,
    send_sta, send_cel, w_full, v_full, station_buf, cell_buf, small_right, small_left,
    sta_send, sta_recv, cel_send, cel_recv, sr_send, sr_recv, sl_send, sl_recv,
):
    width, s_dev = now.shape
    c_dev = right_before.shape[1]
    places = {"sta": (lax.axis_index("sta"), n_sta), "cel": (lax.axis_index("cel"), n_cel)}
    cells = float(c_dev * n_cel)
    stations = float(s_dev * n_sta)

    def group(axis):
        me, n = places[axis]
        return [(o, lax.rem(me + o, n)) for o in range(1, n)]

    barrier = pltpu.get_barrier_semaphore()
    for axis in ("sta", "cel"):
        for _, peer in group(axis):
            pl.semaphore_signal(barrier, inc=1, device_id={axis: peer}, device_id_type=MESH)

    def send(axis, o, peer, source, target, sent, received):
        copy = pltpu.make_async_remote_copy(
            src_ref=source, dst_ref=target, send_sem=sent.at[o], recv_sem=received.at[o],
            device_id={axis: peer}, device_id_type=MESH)
        copy.start()
        return copy

    def finish(copies):
        for copy in copies:
            copy.wait()

    def columns(axis, index, extent):
        share = extent // places[axis][1]
        return pl.ds(pl.multiple_of(index * share, 128), share)

    def scatter(axis, step, source, buf, sent, received, produce, half_way):
        me, n = places[axis]
        copies, made, weights = [], [], None
        for position, (o, peer) in enumerate(group(axis) + [(0, me)]):
            span = columns(axis, peer, source.shape[1])
            if produce is not None:
                produce(span)
            made.append((o, peer, span))
            if position < n // 2 and half_way is not None:
                continue
            if weights is None and half_way is not None:
                weights = half_way()
            for o, peer, span in made:
                if weights is not None:
                    values, mixed = weights
                    source[:, span] = combine(mixed, values[:, span])
                if o:
                    copies.append(send(
                        axis, o, peer, source.at[:, span], buf.at[step, me],
                        sent.at[step, 0], received.at[step, 0]))
            made = []
        return copies

    def gather(axis, step, copies, source, full, buf, sent, received):
        me, n = places[axis]
        mine = columns(axis, me, source.shape[1])
        finish(copies)
        total = source[:, mine]
        for o, peer in group(axis):
            total = total + buf[step, peer]
        if axis == "sta":
            total = total * (GAIN * density[:, mine])
        full[step, :, mine] = total
        block = full.at[step, :, mine]
        finish([
            send(axis, o, peer, block, block, sent.at[step, 1], received.at[step, 1])
            for o, peer in group(axis)
        ])

    def small_start(axis, step, z, buf, sent, received):
        me, n = places[axis]
        rows = z.shape[0]
        buf[step, me, :rows, :rows] = self_products(z)
        block = buf.at[step, me]
        return [send(axis, o, peer, block, block, sent.at[step], received.at[step]) for o, peer in group(axis)]

    def small_end(copies, step, rows, buf, count):
        finish(copies)
        total = buf[step, 0, :rows, :rows]
        for index in range(1, buf.shape[1]):
            total = total + buf[step, index, :rows, :rows]
        return combination(total[:width], total[width:, width:], count)

    station_features(fs, plane, height)
    cell_features(c_square, c_top, cell_plane, depth)
    high, low = split(now[...])
    lhs[:width], lhs[2 * width : 3 * width] = high, low
    high, low = split(before[...])
    lhs[width : 2 * width], lhs[3 * width :] = high, low
    gp[...] = jnp.zeros_like(gp)
    s_tile, c_tile = 256, 512

    def make_rows(index, carry):
        rows = pl.ds(pl.multiple_of(index * s_tile, s_tile), s_tile)
        feature = fs[:, rows].astype(BF16)
        for start in range(0, c_dev, c_tile):
            cols = slice(start, start + c_tile)
            square = dot(feature, c_square[:, cols].astype(BF16), TN)
            top = dot(feature, c_top[:, cols].astype(BF16), TN)
            inverse = lax.rsqrt(square)
            two = inverse * inverse
            high, low = split(two * two * (top * inverse))
            g_high[rows, cols] = high
            g_low[rows, cols] = low
            first = dot(lhs[:, rows], high, NN)
            gp[: 2 * width, cols] += (
                first[: 2 * width] + first[2 * width :] + dot(lhs[: 2 * width, rows], low, NN)
            )
        return carry

    lax.fori_loop(0, s_dev // s_tile, make_rows, 0)
    send_sta[...] = gp[:width]
    gp[2 * width :] = gp[:width]
    pl.semaphore_wait(barrier, n_sta + n_cel - 2)
    copies = scatter("sta", 0, send_sta, station_buf, sta_send, sta_recv, None, None)

    for step in range(STEPS):
        gather("sta", step, copies, send_sta, w_full, station_buf, sta_send, sta_recv)
        w = w_full[step]
        z_right[:width] = w
        if step == 0:
            z_right[width : 2 * width] = right_before[...]
        r_rows = (step + 2) * width
        small = small_start("cel", step, z_right[:r_rows], small_right, sr_send, sr_recv)
        gained = GAIN * density[...]
        high, low = split(w * gained)
        rhs[:width], rhs[2 * width : 3 * width] = high, low
        if step == 0:
            high, low = split(right_before[...] * gained)
            rhs[width : 2 * width], rhs[3 * width :] = high, low

        def forward_share(span):
            first = dot(rhs[...], g_high[span, :], NT)
            second = dot(rhs[: 2 * width], g_low[span, :], NT)
            both = first[: 2 * width] + first[2 * width :] + second
            if step == 0:
                forward[: 2 * width, span] = both
            else:
                forward[:width, span] = both[:width]

        def right_half_way():
            weights, lower = small_end(small, step, r_rows, small_right, cells)
            alphas[step] = lower
            right = combine(weights, z_right[:r_rows])
            rights[step] = right
            if step + 1 < STEPS:
                z_right[r_rows : r_rows + width] = right
            return forward.at[:r_rows], weights

        copies = scatter(
            "cel", step, send_cel, cell_buf, cel_send, cel_recv, forward_share, right_half_way)
        if step + 1 < STEPS:
            forward[r_rows : r_rows + width] = send_cel[...]

        gather("cel", step, copies, send_cel, v_full, cell_buf, cel_send, cel_recv)
        v = v_full[step]
        z_left[:width] = v
        if step == 0:
            z_left[width : 2 * width] = before[...]
            z_left[2 * width : 3 * width] = now[...]
        l_rows = (step + 3) * width
        small = small_start("sta", step, z_left[:l_rows], small_left, sl_send, sl_recv)

        def left_half_way():
            weights, lower = small_end(small, step, l_rows, small_left, stations)
            betas[step] = lower
            block = combine(weights, z_left[:l_rows])
            if step + 1 < STEPS:
                z_left[l_rows : l_rows + width] = block
            else:
                left[...] = block
            return gp.at[:l_rows], weights

        if step + 1 == STEPS:
            left_half_way()
            break
        high, low = split(v)
        lhs[:width], lhs[width : 2 * width] = high, low

        def adjoint_share(span):
            first = dot(lhs[: 2 * width], g_high[:, span], NN)
            second = dot(lhs[:width], g_low[:, span], NN)
            gp[:width, span] = first[:width] + first[width:] + second

        copies = scatter(
            "sta", step + 1, send_sta, station_buf, sta_send, sta_recv, adjoint_share, left_half_way)
        if step + 2 < STEPS:
            gp[l_rows : l_rows + width] = send_sta[...]


def body(plane, height, cell_plane, depth, density, before, now, right_before):
    width, s_dev = now.shape
    c_dev = right_before.shape[1]
    n_sta = lax.axis_size("sta")
    n_cel = lax.axis_size("cel")
    vmem = pl.BlockSpec(memory_space=pltpu.VMEM)
    dma = pltpu.SemaphoreType.DMA
    lanes = 128
    out_shape = (
        jax.ShapeDtypeStruct((STEPS, width, c_dev), F32),
        jax.ShapeDtypeStruct((width, s_dev), F32),
        jax.ShapeDtypeStruct((STEPS, width, width), F32),
        jax.ShapeDtypeStruct((STEPS, width, width), F32),
    )
    scratch = [
        pltpu.VMEM((s_dev, c_dev), BF16),
        pltpu.VMEM((s_dev, c_dev), BF16),
        pltpu.VMEM((FEATURES, s_dev), F32),
        pltpu.VMEM((FEATURES, c_dev), F32),
        pltpu.VMEM((FEATURES, c_dev), F32),
        pltpu.VMEM((4 * width, s_dev), BF16),
        pltpu.VMEM(((STEPS + 1) * width, c_dev), F32),
        pltpu.VMEM(((STEPS + 1) * width, s_dev), F32),
        pltpu.VMEM((4 * width, c_dev), BF16),
        pltpu.VMEM(((STEPS + 1) * width, c_dev), F32),
        pltpu.VMEM(((STEPS + 2) * width, s_dev), F32),
        pltpu.VMEM((width, c_dev), F32),
        pltpu.VMEM((width, s_dev), F32),
        pltpu.VMEM((STEPS, width, c_dev), F32),
        pltpu.VMEM((STEPS, width, s_dev), F32),
        pltpu.VMEM((STEPS, n_sta, width, c_dev // n_sta), F32),
        pltpu.VMEM((STEPS, n_cel, width, s_dev // n_cel), F32),
        pltpu.VMEM((STEPS, n_cel, (STEPS + 1) * width, lanes), F32),
        pltpu.VMEM((STEPS, n_sta, (STEPS + 2) * width, lanes), F32),
        dma((STEPS, 2, n_sta)),
        dma((STEPS, 2, n_sta)),
        dma((STEPS, 2, n_cel)),
        dma((STEPS, 2, n_cel)),
        dma((STEPS, n_cel)),
        dma((STEPS, n_cel)),
        dma((STEPS, n_sta)),
        dma((STEPS, n_sta)),
    ]
    return pl.pallas_call(
        functools.partial(kernel, n_sta, n_cel),
        out_shape=out_shape,
        in_specs=[vmem] * 8,
        out_specs=(vmem,) * 4,
        scratch_shapes=scratch,
        compiler_params=pltpu.CompilerParams(
            collective_id=0, has_side_effects=True, vmem_limit_bytes=56 * 1024 * 1024
        ),
        cost_estimate=pl.CostEstimate(
            flops=2 * 3 * 2 * STEPS * width * s_dev * c_dev, bytes_accessed=4 * 1024 * 1024, transcendentals=s_dev * c_dev
        ),
    )(plane, height[None, :], cell_plane, depth[None, :], density[None, :], before, now, right_before)


def solution(mesh):
    in_specs = (
        P(None, "sta"),
        P("sta"),
        P(None, "cel"),
        P("cel"),
        P("cel"),
        P(None, "sta"),
        P(None, "sta"),
        P(None, "cel"),
    )
    out_specs = (P(None, None, "cel"), P(None, "sta"), P(), P())
    return jax.shard_map(body, mesh=mesh, in_specs=in_specs, out_specs=out_specs, check_vma=False)
```

time: 141 us -> 113 us (0.80)
  Pallas kernels: 129 us -> 108 us
  local copies, waits for them, and re-layouts: 9.48 us -> 3.76 us
  other arithmetic: 1.5 us -> 0 us
    pallas_call x1, Pallas kernels: 129 us -> 108 us  [body(): pl.pallas_call(functools.partial(kernel, n_sta, n_cel), out_shape=out_sha...]
    another operation x20 -> x0, local copies, waits for them, and re-layouts: 4.37 us -> none  [the longest x5 1.55 us: station_features(): return jnp.stack(rows).astype(BF16)]
    unnamed x18 -> x10, local copies, waits for them, and re-layouts: 5.11 us -> 3.76 us
where the time goes in v2:
time: 113 us
  Pallas kernels  108 us (96%)
  local copies, waits for them, and re-layouts  3.76 us (3%)
    pallas_call x1, Pallas kernels, body(): pl.pallas_call(functools.partial(kernel, n_sta, n_cel), out_shape=out_sha...  108 us
    unnamed x10, local copies, waits for them, and re-layouts  3.76 us

profile of v2, /device:TPU:0, one launch (start us, length us, event | category | flops | bytes accessed | tf_op | source)
XLA Modules:
  0.0 112.7 jit_solution(10289038111112446408)
XLA Ops:
  0.6 108.3 %shard_map.111 = (f32[2,16,2048]{2,1,0:T(8,128)}, f32[16,4096]{1,0:T(8,128)}, f32[2,16,16]{2,1,0:T(8,128)}, f32[2,16,16]{2,1,0:T(8,128)}) custom-call(s32[2,4096]{1,0:T(2,128)} %plane.1, s32[1,4096]{1,0:T(1,128)} %bitcast.3, s32[2,2048]{1,0:T(2,128)} %cell_plane.1, s32[1,2048]{1,0:T(1,128)} %bitcast.4, f32[1,2048]{1,0:T(1,128)} %bitcast.5, ...), custom_call_target="tpu_custom_call" | custom-call | flops 3221225472 | bytes 4194304 | tf_op jit(solution)/shard_map/pallas_call | solution.py:349
  108.9 0.0 copy-start
  108.9 1.7 %copy.16 = f32[2,16,2048]{2,1,0:T(8,128)} copy(f32[2,16,2048]{2,1,0:T(8,128)} %get-tuple-element.8) | data formatting | bytes 524288
  110.6 0.0 copy-done
  110.6 0.0 copy-start.2
  110.6 0.7 copy.17
  111.3 0.0 copy-done.2
  111.3 0.0 copy-start.1
  111.3 0.6 copy.18
  111.9 0.1 copy-done.1
  112.1 0.6 copy.19
Async XLA Ops:
  108.9 1.7 %copy-start = (f32[16,4096]{1,0:T(8,128)S(1)}, f32[16,4096]{1,0:T(8,128)}, u32[]{:S(2)}) copy-start(f32[16,4096]{1,0:T(8,128)} %get-tuple-element.9) | copy-start | bytes 786436
  110.6 0.7 copy-start.2
  111.3 0.7 copy-start.1

commit v3 on v2

--- a/solution.py
+++ b/solution.py
@@ -93,9 +93,22 @@
     return weights, lower
 
 
-def self_products(values):
+def products(values, count):
     high, low = split(values)
-    return dot(high, high, NT) + dot(high, low, NT) + dot(low, high, NT)
+    return dot(high[:count], high, NT) + dot(high[:count], low, NT) + dot(low[:count], high, NT)
+
+
+def grow(gram, weights, cross, rows):
+    width, span = cross.shape
+    basis = gram[:span, :span]
+    side = dot(weights[:, :width], cross, NN, HIGH) + dot(weights[:, width:], basis, NN, HIGH)
+    edge = span + width
+    row = lax.broadcasted_iota(jnp.int32, (span, span), 0)
+    col = lax.broadcasted_iota(jnp.int32, (span, span), 1)
+    eye = (row == col).astype(F32)
+    gram[span:edge, :span] = side
+    gram[:span, span:edge] = dot(eye, side, NT, HIGH)
+    gram[span:edge, span:edge] = eye[:width, :width] * rows
 
 
 def combine(weights, values):
@@ -110,8 +123,9 @@
     n_sta, n_cel, plane, height, cell_plane, depth, density, before, now, right_before,
     rights, left, alphas, betas,
     g_high, g_low, fs, c_square, c_top, lhs, gp, forward, rhs, z_right, z_left,
-    send_sta, send_cel, w_full, v_full, station_buf, cell_buf, small_right, small_left,
-    sta_send, sta_recv, cel_send, cel_recv, sr_send, sr_recv, sl_send, sl_recv,
+    send_sta, send_cel, w_full, v_full, station_buf, cell_buf, small_right, small_share, small_left,
+    gram_right, gram_left,
+    sta_send, sta_recv, cel_send, cel_recv, sr_send, sr_recv, ss_send, ss_recv, sl_send, sl_recv,
 ):
     width, s_dev = now.shape
     c_dev = right_before.shape[1]
@@ -166,35 +180,46 @@
             made = []
         return copies
 
-    def gather(axis, step, copies, source, full, buf, sent, received):
+    def reduced(axis, step, copies, source, buf):
         me, n = places[axis]
-        mine = columns(axis, me, source.shape[1])
         finish(copies)
-        total = source[:, mine]
+        total = source[:, columns(axis, me, source.shape[1])]
         for o, peer in group(axis):
             total = total + buf[step, peer]
-        if axis == "sta":
-            total = total * (GAIN * density[:, mine])
-        full[step, :, mine] = total
-        block = full.at[step, :, mine]
-        finish([
+        return total
+
+    def gather(axis, step, full, total, sent, received):
+        span = columns(axis, places[axis][0], full.shape[2])
+        full[step, :, span] = total
+        block = full.at[step, :, span]
+        return [
             send(axis, o, peer, block, block, sent.at[step, 1], received.at[step, 1])
             for o, peer in group(axis)
-        ])
-
-    def small_start(axis, step, z, buf, sent, received):
+        ]
+
+    def exchange(axis, step, values, buf, sent, received):
         me, n = places[axis]
-        rows = z.shape[0]
-        buf[step, me, :rows, :rows] = self_products(z)
-        block = buf.at[step, me]
-        return [send(axis, o, peer, block, block, sent.at[step], received.at[step]) for o, peer in group(axis)]
-
-    def small_end(copies, step, rows, buf, count):
+        rows, cols = values.shape
+        buf[step, me, :rows, :cols] = values
+        block = buf.at[step, me, :rows]
+        return [
+            send(axis, o, peer, block, block, sent.at[step], received.at[step])
+            for o, peer in group(axis)
+        ]
+
+    def collect(copies, step, rows, cols, buf):
         finish(copies)
-        total = buf[step, 0, :rows, :rows]
+        total = buf[step, 0, :rows, :cols]
         for index in range(1, buf.shape[1]):
-            total = total + buf[step, index, :rows, :rows]
-        return combination(total[:width], total[width:, width:], count)
+            total = total + buf[step, index, :rows, :cols]
+        return total
+
+    def solve(step, sums, gram, count, lowers):
+        span = sums.shape[1] - width
+        if step == 0:
+            gram[:span, :span] = sums[width:, width:]
+        weights, lowers[step] = combination(sums[:width], gram[:span, :span], count)
+        return weights
 
     station_features(fs, plane, height)
     cell_features(c_square, c_top, cell_plane, depth)
@@ -229,14 +254,20 @@
     pl.semaphore_wait(barrier, n_sta + n_cel - 2)
     copies = scatter("sta", 0, send_sta, station_buf, sta_send, sta_recv, None, None)
 
+    c_me = places["cel"][0]
     for step in range(STEPS):
-        gather("sta", step, copies, send_sta, w_full, station_buf, sta_send, sta_recv)
+        last = step + 1 == STEPS
+        total = reduced("sta", step, copies, send_sta, station_buf)
+        total = total * (GAIN * density[:, columns("sta", places["sta"][0], c_dev)])
+        finish(gather("sta", step, w_full, total, sta_send, sta_recv))
         w = w_full[step]
         z_right[:width] = w
         if step == 0:
             z_right[width : 2 * width] = right_before[...]
         r_rows = (step + 2) * width
-        small = small_start("cel", step, z_right[:r_rows], small_right, sr_send, sr_recv)
+        r_sent = width if step else r_rows
+        small = exchange(
+            "cel", step, products(z_right[:r_rows], r_sent), small_right, sr_send, sr_recv)
         gained = GAIN * density[...]
         high, low = split(w * gained)
         rhs[:width], rhs[2 * width : 3 * width] = high, low
@@ -253,52 +284,90 @@
             else:
                 forward[:width, span] = both[:width]
 
+        right_sums = []
+
         def right_half_way():
-            weights, lower = small_end(small, step, r_rows, small_right, cells)
-            alphas[step] = lower
-            right = combine(weights, z_right[:r_rows])
-            rights[step] = right
-            if step + 1 < STEPS:
-                z_right[r_rows : r_rows + width] = right
+            sums = collect(small, step, r_sent, r_rows, small_right)
+            right_sums.append(sums)
+            weights = solve(step, sums, gram_right, cells, alphas)
+            right_sums.append(weights)
             return forward.at[:r_rows], weights
 
         copies = scatter(
             "cel", step, send_cel, cell_buf, cel_send, cel_recv, forward_share, right_half_way)
-        if step + 1 < STEPS:
+        sums, weights = right_sums
+        right = combine(weights, z_right[:r_rows])
+        rights[step] = right
+        if not last:
+            z_right[r_rows : r_rows + width] = right
             forward[r_rows : r_rows + width] = send_cel[...]
-
-        gather("cel", step, copies, send_cel, v_full, cell_buf, cel_send, cel_recv)
-        v = v_full[step]
-        z_left[:width] = v
+            grow(gram_right, weights, sums[:width, width:], cells)
         if step == 0:
             z_left[width : 2 * width] = before[...]
             z_left[2 * width : 3 * width] = now[...]
+
+        total = reduced("cel", step, copies, send_cel, cell_buf)
+        mine = columns("cel", c_me, s_dev)
+        z_left[:width, mine] = total
         l_rows = (step + 3) * width
-        small = small_start("sta", step, z_left[:l_rows], small_left, sl_send, sl_recv)
+        l_sent = width if step else l_rows
+        shared = exchange(
+            "cel", step, products(z_left[:l_rows, mine], l_sent), small_share, ss_send, ss_recv)
+        arriving = gather("cel", step, v_full, total, cel_send, cel_recv)
+
+        def left_exchange():
+            sums = collect(shared, step, l_sent, l_rows, small_share)
+            return exchange("sta", step, sums, small_left, sl_send, sl_recv)
+
+        if last:
+            small = left_exchange()
+            finish(arriving)
+            z_left[:width] = v_full[step]
+            sums = collect(small, step, l_sent, l_rows, small_left)
+            left[...] = combine(solve(step, sums, gram_left, stations, betas), z_left[:l_rows])
+            break
+
+        def adjoint(rows, span):
+            first = dot(lhs[: 2 * width, rows], g_high[rows, span], NN)
+            return first[:width] + first[width:] + dot(lhs[:width, rows], g_low[rows, span], NN)
+
+        def load(rows):
+            high, low = split(v_full[step, :, rows])
+            lhs[:width, rows], lhs[width : 2 * width, rows] = high, low
+
+        load(mine)
+        for start in range(0, c_dev, c_tile):
+            span = slice(start, start + c_tile)
+            gp[:width, span] = adjoint(mine, span)
+        small = left_exchange()
+        rows = mine
+        for o, copy in enumerate(arriving, 1):
+            copy.wait()
+            rows = columns("cel", lax.rem(c_me + n_cel - o, n_cel), s_dev)
+            load(rows)
+            if o + 1 < n_cel:
+                for start in range(0, c_dev, c_tile):
+                    span = slice(start, start + c_tile)
+                    gp[:width, span] += adjoint(rows, span)
+        z_left[:width] = v_full[step]
+
+        def adjoint_share(span):
+            gp[:width, span] += adjoint(rows, span)
+
+        left_sums = []
 
         def left_half_way():
-            weights, lower = small_end(small, step, l_rows, small_left, stations)
-            betas[step] = lower
-            block = combine(weights, z_left[:l_rows])
-            if step + 1 < STEPS:
-                z_left[l_rows : l_rows + width] = block
-            else:
-                left[...] = block
+            sums = collect(small, step, l_sent, l_rows, small_left)
+            left_sums.append(sums)
+            weights = solve(step, sums, gram_left, stations, betas)
+            left_sums.append(weights)
             return gp.at[:l_rows], weights
-
-        if step + 1 == STEPS:
-            left_half_way()
-            break
-        high, low = split(v)
-        lhs[:width], lhs[width : 2 * width] = high, low
-
-        def adjoint_share(span):
-            first = dot(lhs[: 2 * width], g_high[:, span], NN)
-            second = dot(lhs[:width], g_low[:, span], NN)
-            gp[:width, span] = first[:width] + first[width:] + second
 
         copies = scatter(
             "sta", step + 1, send_sta, station_buf, sta_send, sta_recv, adjoint_share, left_half_way)
+        sums, weights = left_sums
+        z_left[l_rows : l_rows + width] = combine(weights, z_left[:l_rows])
+        grow(gram_left, weights, sums[:width, width:], stations)
         if step + 2 < STEPS:
             gp[l_rows : l_rows + width] = send_sta[...]
 
@@ -336,11 +405,16 @@
         pltpu.VMEM((STEPS, n_sta, width, c_dev // n_sta), F32),
         pltpu.VMEM((STEPS, n_cel, width, s_dev // n_cel), F32),
         pltpu.VMEM((STEPS, n_cel, (STEPS + 1) * width, lanes), F32),
+        pltpu.VMEM((STEPS, n_cel, (STEPS + 2) * width, lanes), F32),
         pltpu.VMEM((STEPS, n_sta, (STEPS + 2) * width, lanes), F32),
+        pltpu.VMEM(((STEPS + 1) * width, lanes), F32),
+        pltpu.VMEM(((STEPS + 2) * width, lanes), F32),
         dma((STEPS, 2, n_sta)),
         dma((STEPS, 2, n_sta)),
         dma((STEPS, 2, n_cel)),
         dma((STEPS, 2, n_cel)),
+        dma((STEPS, n_cel)),
+        dma((STEPS, n_cel)),
         dma((STEPS, n_cel)),
         dma((STEPS, n_cel)),
         dma((STEPS, n_sta)),

time: 113 us -> 108 us (0.956)
  Pallas kernels: 108 us -> 103 us
    pallas_call x1, Pallas kernels: 108 us -> 103 us  [body(): pl.pallas_call(functools.partial(kernel, n_sta, n_cel), out_shape=out_sha...]
where the time goes in v3:
time: 108 us
  Pallas kernels  103 us (95%)
  local copies, waits for them, and re-layouts  3.76 us (3%)
    pallas_call x1, Pallas kernels, body(): pl.pallas_call(functools.partial(kernel, n_sta, n_cel), out_shape=out_sha...  103 us
    unnamed x10, local copies, waits for them, and re-layouts  3.76 us

profile of v3, /device:TPU:0, one launch (start us, length us, event | category | flops | bytes accessed | tf_op | source)
XLA Modules:
  0.0 107.8 jit_solution(14439215937239783026)
XLA Ops:
  0.6 103.4 %shard_map.111 = (f32[2,16,2048]{2,1,0:T(8,128)}, f32[16,4096]{1,0:T(8,128)}, f32[2,16,16]{2,1,0:T(8,128)}, f32[2,16,16]{2,1,0:T(8,128)}) custom-call(s32[2,4096]{1,0:T(2,128)} %plane.1, s32[1,4096]{1,0:T(1,128)} %bitcast.3, s32[2,2048]{1,0:T(2,128)} %cell_plane.1, s32[1,2048]{1,0:T(1,128)} %bitcast.4, f32[1,2048]{1,0:T(1,128)} %bitcast.5, ...), custom_call_target="tpu_custom_call" | custom-call | flops 3221225472 | bytes 4194304 | tf_op jit(solution)/shard_map/pallas_call | solution.py:423
  104.0 0.0 copy-start
  104.0 1.7 %copy.16 = f32[2,16,2048]{2,1,0:T(8,128)} copy(f32[2,16,2048]{2,1,0:T(8,128)} %get-tuple-element.8) | data formatting | bytes 524288
  105.7 0.0 copy-done
  105.7 0.0 copy-start.2
  105.7 0.7 copy.17
  106.4 0.0 copy-done.2
  106.4 0.0 copy-start.1
  106.4 0.6 copy.18
  107.0 0.1 copy-done.1
  107.2 0.6 copy.19
Async XLA Ops:
  104.0 1.7 %copy-start = (f32[16,4096]{1,0:T(8,128)S(1)}, f32[16,4096]{1,0:T(8,128)}, u32[]{:S(2)}) copy-start(f32[16,4096]{1,0:T(8,128)} %get-tuple-element.9) | copy-start | bytes 786436
  105.7 0.7 copy-start.2
  106.4 0.7 copy-start.1

commit v4 on v3

--- a/solution.py
+++ b/solution.py
@@ -228,24 +228,37 @@
     high, low = split(before[...])
     lhs[width : 2 * width], lhs[3 * width :] = high, low
     gp[...] = jnp.zeros_like(gp)
-    s_tile, c_tile = 256, 512
+    s_tile, c_tile, g_tile, g_chunk = 256, 512, 256, 32
 
     def make_rows(index, carry):
         rows = pl.ds(pl.multiple_of(index * s_tile, s_tile), s_tile)
         feature = fs[:, rows].astype(BF16)
-        for start in range(0, c_dev, c_tile):
-            cols = slice(start, start + c_tile)
+
+        def multiply(cols):
+            first = dot(lhs[:, rows], g_high[rows, cols], NN)
+            gp[: 2 * width, cols] += (
+                first[: 2 * width]
+                + first[2 * width :]
+                + dot(lhs[: 2 * width, rows], g_low[rows, cols], NN)
+            )
+
+        previous = None
+        for start in range(0, c_dev, g_tile):
+            cols = slice(start, start + g_tile)
             square = dot(feature, c_square[:, cols].astype(BF16), TN)
             top = dot(feature, c_top[:, cols].astype(BF16), TN)
-            inverse = lax.rsqrt(square)
-            two = inverse * inverse
-            high, low = split(two * two * (top * inverse))
-            g_high[rows, cols] = high
-            g_low[rows, cols] = low
-            first = dot(lhs[:, rows], high, NN)
-            gp[: 2 * width, cols] += (
-                first[: 2 * width] + first[2 * width :] + dot(lhs[: 2 * width, rows], low, NN)
-            )
+            for chunk in range(0, s_tile, g_chunk):
+                part = slice(chunk, chunk + g_chunk)
+                inverse = lax.rsqrt(square[part])
+                two = inverse * inverse
+                high, low = split(two * two * (top[part] * inverse))
+                at = pl.ds(pl.multiple_of(index * s_tile + chunk, g_chunk), g_chunk)
+                g_high[at, cols] = high
+                g_low[at, cols] = low
+            if previous is not None:
+                multiply(previous)
+            previous = cols
+        multiply(previous)
         return carry
 
     lax.fori_loop(0, s_dev // s_tile, make_rows, 0)

time: 108 us -> 119 us (1.10)
  Pallas kernels: 103 us -> 114 us
    pallas_call x1, Pallas kernels: 103 us -> 114 us  [body(): pl.pallas_call(functools.partial(kernel, n_sta, n_cel), out_shape=out_sha...]
where the time goes in v4:
time: 119 us
  Pallas kernels  114 us (96%)
  local copies, waits for them, and re-layouts  3.76 us (3%)
    pallas_call x1, Pallas kernels, body(): pl.pallas_call(functools.partial(kernel, n_sta, n_cel), out_shape=out_sha...  114 us
    unnamed x10, local copies, waits for them, and re-layouts  3.76 us

profile of v4, /device:TPU:0, one launch (start us, length us, event | category | flops | bytes accessed | tf_op | source)
XLA Modules:
  0.0 118.8 jit_solution(8547401248603168534)
XLA Ops:
  0.6 114.4 %shard_map.111 = (f32[2,16,2048]{2,1,0:T(8,128)}, f32[16,4096]{1,0:T(8,128)}, f32[2,16,16]{2,1,0:T(8,128)}, f32[2,16,16]{2,1,0:T(8,128)}) custom-call(s32[2,4096]{1,0:T(2,128)} %plane.1, s32[1,4096]{1,0:T(1,128)} %bitcast.3, s32[2,2048]{1,0:T(2,128)} %cell_plane.1, s32[1,2048]{1,0:T(1,128)} %bitcast.4, f32[1,2048]{1,0:T(1,128)} %bitcast.5, ...), custom_call_target="tpu_custom_call" | custom-call | flops 3221225472 | bytes 4194304 | tf_op jit(solution)/shard_map/pallas_call | solution.py:436
  115.1 0.0 copy-start
  115.1 1.7 %copy.16 = f32[2,16,2048]{2,1,0:T(8,128)} copy(f32[2,16,2048]{2,1,0:T(8,128)} %get-tuple-element.8) | data formatting | bytes 524288
  116.8 0.0 copy-done
  116.8 0.0 copy-start.2
  116.8 0.7 copy.17
  117.5 0.0 copy-done.2
  117.5 0.0 copy-start.1
  117.5 0.6 copy.18
  118.1 0.1 copy-done.1
  118.2 0.6 copy.19
Async XLA Ops:
  115.1 1.7 %copy-start = (f32[16,4096]{1,0:T(8,128)S(1)}, f32[16,4096]{1,0:T(8,128)}, u32[]{:S(2)}) copy-start(f32[16,4096]{1,0:T(8,128)} %get-tuple-element.9) | copy-start | bytes 786436
  116.8 0.7 copy-start.2
  117.5 0.7 copy-start.1

commit v5 on v3

--- a/solution.py
+++ b/solution.py
@@ -122,7 +122,7 @@
 def kernel(
     n_sta, n_cel, plane, height, cell_plane, depth, density, before, now, right_before,
     rights, left, alphas, betas,
-    g_high, g_low, fs, c_square, c_top, lhs, gp, forward, rhs, z_right, z_left,
+    g_high, g_low, fs, turned, c_square, c_top, lhs, gp, forward, rhs, z_right, z_left,
     send_sta, send_cel, w_full, v_full, station_buf, cell_buf, small_right, small_share, small_left,
     gram_right, gram_left,
     sta_send, sta_recv, cel_send, cel_recv, sr_send, sr_recv, ss_send, ss_recv, sl_send, sl_recv,
@@ -227,28 +227,35 @@
     lhs[:width], lhs[2 * width : 3 * width] = high, low
     high, low = split(before[...])
     lhs[width : 2 * width], lhs[3 * width :] = high, low
-    gp[...] = jnp.zeros_like(gp)
-    s_tile, c_tile = 256, 512
-
-    def make_rows(index, carry):
-        rows = pl.ds(pl.multiple_of(index * s_tile, s_tile), s_tile)
-        feature = fs[:, rows].astype(BF16)
-        for start in range(0, c_dev, c_tile):
-            cols = slice(start, start + c_tile)
-            square = dot(feature, c_square[:, cols].astype(BF16), TN)
-            top = dot(feature, c_top[:, cols].astype(BF16), TN)
+    row = lax.broadcasted_iota(jnp.int32, (FEATURES, FEATURES), 0)
+    col = lax.broadcasted_iota(jnp.int32, (FEATURES, FEATURES), 1)
+    eye = (row == col).astype(BF16)
+    s_tile, c_tile, g_tile = min(1024, s_dev), 512, 256
+    for start in range(0, s_dev, s_tile):
+        rows = slice(start, start + s_tile)
+        turned[rows, :] = dot(fs[:, rows].astype(BF16), eye, TN).astype(BF16)
+
+    def make_columns(index, carry):
+        cols = pl.ds(pl.multiple_of(index * g_tile, g_tile), g_tile)
+        total = jnp.zeros((2 * width, g_tile), F32)
+        c_low, c_high = c_square[:, cols].astype(BF16), c_top[:, cols].astype(BF16)
+        for start in range(0, s_dev, s_tile):
+            rows = slice(start, start + s_tile)
+            square = dot(turned[rows, :], c_low, NN)
+            top = dot(turned[rows, :], c_high, NN)
             inverse = lax.rsqrt(square)
             two = inverse * inverse
             high, low = split(two * two * (top * inverse))
             g_high[rows, cols] = high
             g_low[rows, cols] = low
             first = dot(lhs[:, rows], high, NN)
-            gp[: 2 * width, cols] += (
+            total = total + (
                 first[: 2 * width] + first[2 * width :] + dot(lhs[: 2 * width, rows], low, NN)
             )
+        gp[: 2 * width, cols] = total
         return carry
 
-    lax.fori_loop(0, s_dev // s_tile, make_rows, 0)
+    lax.fori_loop(0, c_dev // g_tile, make_columns, 0)
     send_sta[...] = gp[:width]
     gp[2 * width :] = gp[:width]
     pl.semaphore_wait(barrier, n_sta + n_cel - 2)
@@ -390,6 +397,7 @@
         pltpu.VMEM((s_dev, c_dev), BF16),
         pltpu.VMEM((s_dev, c_dev), BF16),
         pltpu.VMEM((FEATURES, s_dev), F32),
+        pltpu.VMEM((s_dev, FEATURES), BF16),
         pltpu.VMEM((FEATURES, c_dev), F32),
         pltpu.VMEM((FEATURES, c_dev), F32),
         pltpu.VMEM((4 * width, s_dev), BF16),

time: 108 us -> 105 us (0.972)
  Pallas kernels: 103 us -> 100 us
    pallas_call x1, Pallas kernels: 103 us -> 100 us  [body(): pl.pallas_call(functools.partial(kernel, n_sta, n_cel), out_shape=out_sha...]
where the time goes in v5:
time: 105 us
  Pallas kernels  100 us (95%)
  local copies, waits for them, and re-layouts  3.76 us (4%)
    pallas_call x1, Pallas kernels, body(): pl.pallas_call(functools.partial(kernel, n_sta, n_cel), out_shape=out_sha...  100 us
    unnamed x10, local copies, waits for them, and re-layouts  3.76 us

profile of v5, /device:TPU:0, one launch (start us, length us, event | category | flops | bytes accessed | tf_op | source)
XLA Modules:
  0.0 104.5 jit_solution(15948632393898569599)
XLA Ops:
  0.6 100.1 %shard_map.111 = (f32[2,16,2048]{2,1,0:T(8,128)}, f32[16,4096]{1,0:T(8,128)}, f32[2,16,16]{2,1,0:T(8,128)}, f32[2,16,16]{2,1,0:T(8,128)}) custom-call(s32[2,4096]{1,0:T(2,128)} %plane.1, s32[1,4096]{1,0:T(1,128)} %bitcast.3, s32[2,2048]{1,0:T(2,128)} %cell_plane.1, s32[1,2048]{1,0:T(1,128)} %bitcast.4, f32[1,2048]{1,0:T(1,128)} %bitcast.5, ...), custom_call_target="tpu_custom_call" | custom-call | flops 3221225472 | bytes 4194304 | tf_op jit(solution)/shard_map/pallas_call | solution.py:431
  100.7 0.0 copy-start
  100.7 1.7 %copy.16 = f32[2,16,2048]{2,1,0:T(8,128)} copy(f32[2,16,2048]{2,1,0:T(8,128)} %get-tuple-element.8) | data formatting | bytes 524288
  102.5 0.0 copy-done
  102.5 0.0 copy-start.2
  102.5 0.7 copy.17
  103.2 0.0 copy-done.2
  103.2 0.0 copy-start.1
  103.2 0.6 copy.18
  103.8 0.1 copy-done.1
  103.9 0.6 copy.19
Async XLA Ops:
  100.7 1.7 %copy-start = (f32[16,4096]{1,0:T(8,128)S(1)}, f32[16,4096]{1,0:T(8,128)}, u32[]{:S(2)}) copy-start(f32[16,4096]{1,0:T(8,128)} %get-tuple-element.9) | copy-start | bytes 786436
  102.5 0.7 copy-start.2
  103.2 0.7 copy-start.1

commit v6 on v5

--- a/solution.py
+++ b/solution.py
@@ -122,7 +122,7 @@
 def kernel(
     n_sta, n_cel, plane, height, cell_plane, depth, density, before, now, right_before,
     rights, left, alphas, betas,
-    g_high, g_low, fs, turned, c_square, c_top, lhs, gp, forward, rhs, z_right, z_left,
+    g_high, g_low, fs, turned, c_square, c_top, lhs, gp, forward, rhs, rhs_low, z_right, z_left,
     send_sta, send_cel, w_full, v_full, station_buf, cell_buf, small_right, small_share, small_left,
     gram_right, gram_left,
     sta_send, sta_recv, cel_send, cel_recv, sr_send, sr_recv, ss_send, ss_recv, sl_send, sl_recv,
@@ -280,12 +280,15 @@
         rhs[:width], rhs[2 * width : 3 * width] = high, low
         if step == 0:
             high, low = split(right_before[...] * gained)
-            rhs[width : 2 * width], rhs[3 * width :] = high, low
+            rhs[width : 2 * width], rhs[3 * width : 4 * width] = high, low
+            rhs[4 * width :] = jnp.zeros((rhs.shape[0] - 4 * width, c_dev), BF16)
+            rhs_low[2 * width :] = jnp.zeros((rhs.shape[0] - 2 * width, c_dev), BF16)
+        rhs_low[: 2 * width] = rhs[: 2 * width]
 
         def forward_share(span):
-            first = dot(rhs[...], g_high[span, :], NT)
-            second = dot(rhs[: 2 * width], g_low[span, :], NT)
-            both = first[: 2 * width] + first[2 * width :] + second
+            first = dot(g_high[span, :], rhs[...], NT) + dot(g_low[span, :], rhs_low[...], NT)
+            first = first.T
+            both = first[: 2 * width] + first[2 * width : 4 * width]
             if step == 0:
                 forward[: 2 * width, span] = both
             else:
@@ -403,7 +406,8 @@
         pltpu.VMEM((4 * width, s_dev), BF16),
         pltpu.VMEM(((STEPS + 1) * width, c_dev), F32),
         pltpu.VMEM(((STEPS + 1) * width, s_dev), F32),
-        pltpu.VMEM((4 * width, c_dev), BF16),
+        pltpu.VMEM((lanes, c_dev), BF16),
+        pltpu.VMEM((lanes, c_dev), BF16),
         pltpu.VMEM(((STEPS + 1) * width, c_dev), F32),
         pltpu.VMEM(((STEPS + 2) * width, s_dev), F32),
         pltpu.VMEM((width, c_dev), F32),

time: 105 us -> 107 us (1.019)
  Pallas kernels: 100 us -> 103 us
    pallas_call x1, Pallas kernels: 100 us -> 103 us  [body(): pl.pallas_call(functools.partial(kernel, n_sta, n_cel), out_shape=out_sha...]
where the time goes in v6:
time: 107 us
  Pallas kernels  103 us (96%)
  local copies, waits for them, and re-layouts  3.76 us (4%)
    pallas_call x1, Pallas kernels, body(): pl.pallas_call(functools.partial(kernel, n_sta, n_cel), out_shape=out_sha...  103 us
    unnamed x10, local copies, waits for them, and re-layouts  3.76 us

profile of v6, /device:TPU:0, one launch (start us, length us, event | category | flops | bytes accessed | tf_op | source)
XLA Modules:
  0.0 106.9 jit_solution(6320505136415795616)
XLA Ops:
  0.6 102.5 %shard_map.111 = (f32[2,16,2048]{2,1,0:T(8,128)}, f32[16,4096]{1,0:T(8,128)}, f32[2,16,16]{2,1,0:T(8,128)}, f32[2,16,16]{2,1,0:T(8,128)}) custom-call(s32[2,4096]{1,0:T(2,128)} %plane.1, s32[1,4096]{1,0:T(1,128)} %bitcast.3, s32[2,2048]{1,0:T(2,128)} %cell_plane.1, s32[1,2048]{1,0:T(1,128)} %bitcast.4, f32[1,2048]{1,0:T(1,128)} %bitcast.5, ...), custom_call_target="tpu_custom_call" | custom-call | flops 3221225472 | bytes 4194304 | tf_op jit(solution)/shard_map/pallas_call | solution.py:435
  103.2 0.0 copy-start
  103.2 1.7 %copy.16 = f32[2,16,2048]{2,1,0:T(8,128)} copy(f32[2,16,2048]{2,1,0:T(8,128)} %get-tuple-element.8) | data formatting | bytes 524288
  104.9 0.0 copy-done
  104.9 0.0 copy-start.2
  104.9 0.7 copy.17
  105.6 0.0 copy-done.2
  105.6 0.0 copy-start.1
  105.6 0.6 copy.18
  106.2 0.1 copy-done.1
  106.3 0.6 copy.19
Async XLA Ops:
  103.2 1.7 %copy-start = (f32[16,4096]{1,0:T(8,128)S(1)}, f32[16,4096]{1,0:T(8,128)}, u32[]{:S(2)}) copy-start(f32[16,4096]{1,0:T(8,128)} %get-tuple-element.9) | copy-start | bytes 786436
  104.9 0.7 copy-start.2
  105.6 0.7 copy-start.1
